TPU v7x, 512 devices: a whole 4x8x8 slice. The times are simulated.
512 devices in a mesh: seq: 128 (over z, y_lo, x, core), tp: 4 (over y_hi).
Axes of the slice: x: 4, y: 8 (y_hi: 4, y_lo: 2; y = y_hi * 2 + y_lo), z: 8, core: 2. Of those that a mesh axis runs over, the one named last changes fastest.
Arguments:
- token_picks: int32 [2560], replicated, may hold values from 0 to 127, as said below
- live_counts: int32 [128, 2], replicated, may hold values from 1 to 16, as said below
- attn_query: bfloat16 [2560, 1024], P('seq', 'tp'), may hold values from -10 to 10
- attn_key: bfloat16 [2560, 1024], P('seq', 'tp'), may hold values from -10 to 10
- attn_value: bfloat16 [2560, 1024], P('seq', 'tp'), may hold values from -6 to 6
- out_grad: bfloat16 [2560, 2048], P('seq', 'tp'), may hold values from -24 to 24
- out_weight: bfloat16 [1024, 2048], P('tp'), may hold values from -0.1875 to 0.1875
Outputs:
- query_grad: bfloat16 [2560, 1024], P('seq', 'tp')
- key_grad: bfloat16 [2560, 1024], P('seq', 'tp')
- value_grad: bfloat16 [2560, 1024], P('seq', 'tp')
- weight_grad: float32 [1024, 2048], P('tp', 'seq')
Inputs may be any that keep to these rules, and one draw needn't show every extreme that they name: `token_picks`: for every index j of seq and each recursion, the first live_counts entries of its list are distinct token positions of shard j in increasing order and the rest are 0; the positions listed for the third recursion are among those listed for the second. `live_counts`: row j holds the used slots of the second and the third recursion of index j; the first lies in 4 to 16 and equals 16 for some j, the second lies in 1 to 4, equals 4 for some j and never exceeds the first.
All inputs are finite; a program needn't handle non-finite values.
Results may differ from a plain program's by a relative error of at most 0.0085.
Values may be sent and summed in bfloat16 or wider, within the bound.
No kernel may reach another device: no remote copies, remote signals or barrier semaphores. Data moves between devices by JAX's collectives and lax.ppermute only.
A program may use at most 64 MiB of HBM per device.

v0:
```python
import jax
import jax.numpy as jnp
from jax import lax
from jax.sharding import PartitionSpec as P

HS = 128
TOK_DEV = 128
CAP2 = 16


def tables(token_picks, live_counts, slot_count):
    row_total = token_picks.shape[0]
    row_order = jnp.arange(row_total, dtype=jnp.int32)
    shard_of = row_order // slot_count
    local_slot = row_order % slot_count
    is_third = local_slot >= CAP2
    within = jnp.where(is_third, local_slot - CAP2, local_slot)
    spread = jnp.repeat(live_counts, slot_count, axis=0, total_repeat_length=row_total)
    row_limit = jnp.where(is_third, spread[:, 1], spread[:, 0])
    return (shard_of * TOK_DEV + token_picks, is_third, within < row_limit)


def permitted(query_side, key_side):
    query_pos, query_third, query_live = query_side
    key_pos, key_third, key_live = key_side
    causal = (key_pos[None, :] <= query_pos[:, None]) | jnp.logical_not(query_live)[:, None]
    return key_live[None, :] & (query_third[:, None] == key_third[None, :]) & causal


def sweep_blocks(stored, step_fn, init_state, slot_count, seq_count):
    shard_group = min(seq_count, 16)
    block_rows = shard_group * slot_count

    def one_block(block_index, state_now):
        begin_row = block_index * block_rows
        pieces = tuple(
            (
                lax.dynamic_slice_in_dim(whole_part, begin_row, block_rows, 0)
                for whole_part in stored
            )
        )
        return step_fn(state_now, pieces, begin_row)

    return lax.fori_loop(0, seq_count // shard_group, one_block, init_state)


def on_device(token_picks, live_counts, attn_query, attn_key, attn_value, out_grad, out_weight):
    slot_count = attn_query.shape[0]
    row_width = attn_query.shape[1]
    head_count = row_width // HS
    score_scale = HS ** (-0.5)
    seq_count = lax.axis_size("seq")
    shard_index = lax.axis_index("seq")
    row_info = tables(token_picks, live_counts, slot_count)

    def rows_of(begin_row, count_rows):
        return tuple(
            (
                lax.dynamic_slice_in_dim(column_info, begin_row, count_rows, 0)
                for column_info in row_info
            )
        )

    own_rows = rows_of(shard_index * slot_count, slot_count)
    full_grad = lax.all_gather(out_grad, "tp", axis=1, tiled=True)
    grad_rows = jnp.where(own_rows[2][:, None], full_grad, jnp.zeros_like(full_grad))
    d_attn = lax.dot_general(
        grad_rows, out_weight, (((1,), (1,)), ((), ())), preferred_element_type=jnp.float32
    ).astype(jnp.bfloat16)

    def split_heads(matrix):
        return matrix.reshape(matrix.shape[0], head_count, HS)

    own_query = split_heads(attn_query)
    own_key = split_heads(attn_key)
    own_value = split_heads(attn_value)
    own_dattn = split_heads(d_attn)

    def masked_scores(query_part, query_info, key_part, key_info):
        scores = (
            jnp.einsum("qhd,khd->hqk", query_part, key_part, preferred_element_type=jnp.float32)
            * score_scale
        )
        return jnp.where(permitted(query_info, key_info)[None], scores, -jnp.inf)

    def stats_step(state_now, pieces, begin_row):
        row_max, row_sum, row_dot = state_now
        key_part = split_heads(pieces[0])
        value_part = split_heads(pieces[1])
        scores = masked_scores(own_query, own_rows, key_part, rows_of(begin_row, key_part.shape[0]))
        dprob = jnp.einsum(
            "qhd,khd->hqk", own_dattn, value_part, preferred_element_type=jnp.float32
        )
        new_max = jnp.maximum(row_max, jnp.max(scores, axis=2))
        rescale = jnp.exp(row_max - new_max)
        weights = jnp.exp(scores - new_max[:, :, None])
        return (
            new_max,
            row_sum * rescale + jnp.sum(weights, axis=2),
            row_dot * rescale + jnp.sum(weights * dprob, axis=2),
        )

    def grad_stepper(log_total, row_delta):

        def grad_step(state_now, pieces, begin_row):
            out_sum, query_sum = state_now
            key_part = split_heads(pieces[0])
            value_part = split_heads(pieces[1])
            scores = masked_scores(
                own_query, own_rows, key_part, rows_of(begin_row, key_part.shape[0])
            )
            prob = jnp.exp(scores - log_total[:, :, None])
            prob_half = prob.astype(jnp.bfloat16)
            out_sum = out_sum + jnp.einsum(
                "hqk,khd->qhd", prob_half, value_part, preferred_element_type=jnp.float32
            )
            dprob = jnp.einsum(
                "qhd,khd->hqk", own_dattn, value_part, preferred_element_type=jnp.float32
            )
            dscore = (prob * (dprob - row_delta[:, :, None])).astype(jnp.bfloat16)
            query_sum = query_sum + jnp.einsum(
                "hqk,khd->qhd", dscore, key_part, preferred_element_type=jnp.float32
            )
            return (out_sum, query_sum)

        return grad_step

    stat_zeros = jnp.zeros((head_count, slot_count), jnp.float32)
    stats_init = (jnp.full((head_count, slot_count), -1e30, jnp.float32), stat_zeros, stat_zeros)
    grad_zeros = jnp.zeros((slot_count, head_count, HS), jnp.float32)
    stored = (
        lax.all_gather(attn_key, "seq", axis=0, tiled=True),
        lax.all_gather(attn_value, "seq", axis=0, tiled=True),
    )
    row_max, row_sum, row_dot = sweep_blocks(stored, stats_step, stats_init, slot_count, seq_count)
    log_total = row_max + jnp.log(row_sum)
    row_delta = row_dot / row_sum
    out_sum, query_sum = sweep_blocks(
        stored, grad_stepper(log_total, row_delta), (grad_zeros, grad_zeros), slot_count, seq_count
    )
    attended = out_sum.astype(jnp.bfloat16).reshape(slot_count, row_width)
    query_grad = (query_sum * score_scale).astype(jnp.bfloat16).reshape(slot_count, row_width)
    log_all, delta_all = (
        lax.all_gather(log_total.T, "seq", axis=0, tiled=True),
        lax.all_gather(row_delta.T, "seq", axis=0, tiled=True),
    )

    def key_side(state_now, pieces, begin_row):
        query_part = split_heads(pieces[0])
        grad_part = split_heads(pieces[1])
        piece_rows = query_part.shape[0]
        log_part = log_all.T
        delta_part = delta_all.T
        scores = masked_scores(query_part, rows_of(begin_row, piece_rows), own_key, own_rows)
        prob = jnp.exp(scores - log_part[:, :, None])
        prob_half = prob.astype(jnp.bfloat16)
        value_sum = jnp.einsum(
            "hqk,qhd->khd", prob_half, grad_part, preferred_element_type=jnp.float32
        )
        dprob = jnp.einsum("qhd,khd->hqk", grad_part, own_value, preferred_element_type=jnp.float32)
        dscore = (prob * (dprob - delta_part[:, :, None])).astype(jnp.bfloat16)
        key_sum = jnp.einsum("hqk,qhd->khd", dscore, query_part, preferred_element_type=jnp.float32)
        return (key_sum, value_sum, piece_rows)

    key_init = (grad_zeros, grad_zeros)
    key_sum, value_sum, piece_rows = key_side(
        key_init,
        (
            lax.all_gather(attn_query, "seq", axis=0, tiled=True),
            lax.all_gather(d_attn, "seq", axis=0, tiled=True),
        ),
        jnp.int32(0),
    )
    key_sum, value_sum = (key_sum, value_sum)
    partial_value = lax.dot_general(
        attended, grad_rows, (((0,), (0,)), ((), ())), preferred_element_type=jnp.float32
    )
    weight_grad = lax.psum_scatter(partial_value, "seq", scatter_dimension=1, tiled=True)
    key_grad = (key_sum * score_scale).astype(jnp.bfloat16).reshape(slot_count, row_width)
    value_grad = value_sum.astype(jnp.bfloat16).reshape(slot_count, row_width)
    return (query_grad, key_grad, value_grad, weight_grad)


def solution(mesh):
    in_specs = (
        P(),
        P(),
        P("seq", "tp"),
        P("seq", "tp"),
        P("seq", "tp"),
        P("seq", "tp"),
        P("tp", None),
    )
    out_specs = (P("seq", "tp"), P("seq", "tp"), P("seq", "tp"), P("tp", "seq"))
    return jax.shard_map(
        on_device, mesh=mesh, in_specs=in_specs, out_specs=out_specs, check_vma=False
    )
```

profile of v0, /device:TPU:1, one launch (start us, length us, event | category | flops | bytes accessed | tf_op | source)
XLA Modules:
  0.0 1454.1 jit_solution(17082652081743828530)
XLA Ops:
  7.2 0.7 all-gather.11.cloned.1.call-update
  8.0 0.7 all-gather.13.cloned.1.call-update
  8.7 0.7 all-gather.15.cloned.1.call-update
  9.4 0.8 copy.41
  10.2 0.7 pad_clamp_fusion
  11.0 4.1 gather_fusion
  15.1 14.2 all_gather.23
  29.4 1.1 slice_reduce_fusion
  30.6 1.0 convolution_convert_fusion
  31.8 0.7 reshape.461
  32.7 197.9 %all-gather.11.cloned.1.call-done = bf16[128,20,256]{2,1,0:T(8,128)(2,1)} async-done(((bf16[1,20,256]{2,1,0:T(8,128)(2,1)}), bf16[128,20,256]{2,1,0:T(8,128)(2,1)}) %all-gather.11.cloned.1.call-update) | async-done | bytes 1310736 | tf_op jit(solution)/shard_map/all_gather | solution.py:133
  230.6 3.3 reshape.479
  233.9 213.4 %all-gather.13.cloned.1.call-done = bf16[128,20,256]{2,1,0:T(8,128)(2,1)} async-done(((bf16[1,20,256]{2,1,0:T(8,128)(2,1)}), bf16[128,20,256]{2,1,0:T(8,128)(2,1)}) %all-gather.13.cloned.1.call-update) | async-done | bytes 1310736 | tf_op jit(solution)/shard_map/all_gather | solution.py:132
  447.3 3.3 reshape.481
  450.6 17.3 %while.39 = (s32[]{:T(128)}, f32[2,20]{1,0:T(2,128)S(1)}, f32[2,20]{1,0:T(2,128)S(1)}, f32[2,20]{1,0:T(2,128)S(1)}, pred[2560]{0:T(1024)(128)(4,1)S(1)}, /*index...) while((s32[]{:T(128)}, f32[2,20]{1,0:T(2,128)S(1)}, ...), condition=%wide.region_4.5_spmd.clone, body=%wide.region_0.4_spmd.clone.sunk | while | flops 6688287 | bytes 1178926 | solution.py:44
  450.6 1.0 dynamic-slice_bitcast_fusion.6
  452.7 1.0 dynamic-slice_bitcast_fusion.6
  454.9 1.0 dynamic-slice_bitcast_fusion.6
  457.1 1.0 dynamic-slice_bitcast_fusion.6
  459.2 1.0 dynamic-slice_bitcast_fusion.6
  461.4 1.0 dynamic-slice_bitcast_fusion.6
  463.5 1.0 dynamic-slice_bitcast_fusion.6
  465.7 1.0 dynamic-slice_bitcast_fusion.6
  467.9 16.6 %while.40 = (s32[]{:T(128)}, f32[20,2,128]{2,0,1:T(8,128)S(1)}, f32[20,2,128]{2,0,1:T(8,128)S(1)}, bf16[2560,256]{1,0:T(8,128)(2,1)}, pred[2560]{0:T(1024)(128)(...) while((s32[]{:T(128)}, f32[20,2,128]{2,0,1:T(8,128)S(1)}, ...), condition=%wide.region_6.7_spmd.clone, body=%wide.region_5.6_spmd.clone.sunk | while | flops 13249287 | bytes 1585974 | solution.py:44
  467.9 1.0 dynamic-slice_bitcast_fusion.7
  469.6 0.3 fusion.132
  470.0 1.0 dynamic-slice_bitcast_fusion.7
  471.7 0.3 fusion.132
  472.0 1.0 dynamic-slice_bitcast_fusion.7
  474.1 1.0 dynamic-slice_bitcast_fusion.7
  476.2 1.0 dynamic-slice_bitcast_fusion.7
  478.3 1.0 dynamic-slice_bitcast_fusion.7
  480.3 1.0 dynamic-slice_bitcast_fusion.7
  482.4 1.0 dynamic-slice_bitcast_fusion.7
  484.5 1.9 fusion.74
  486.5 0.7 copy-done.1
  487.2 1.2 not_reduce_fusion
  488.5 0.6 copy.62
  489.2 154.5 %all-gather.3 = f32[128,20,2]{1,2,0:T(2,128)S(1)} all-gather(f32[1,20,2]{1,2,0:T(2,128)S(1)} %bitcast.162), channel_id=1, replica_groups=mesh['seq'=128,'tp'=4] {'seq'}, dimensions={0}, use_global_device_ids=true | all-gather | bytes 20640 | tf_op jit(solution)/shard_map/all_gather | solution.py:144
  643.8 151.2 %all-gather.5 = f32[128,20,2]{1,2,0:T(2,128)S(1)} all-gather(f32[1,20,2]{1,2,0:T(2,128)S(1)} %bitcast.161), channel_id=1, replica_groups=mesh['seq'=128,'tp'=4] {'seq'}, dimensions={0}, use_global_device_ids=true | all-gather | bytes 20640 | tf_op jit(solution)/shard_map/all_gather | solution.py:145
  795.2 4.0 reshape.463
  799.2 82.2 %all-gather.17.cloned.1.call-done = bf16[128,20,256]{2,1,0:T(8,128)(2,1)} async-done(((bf16[1,20,256]{2,1,0:T(8,128)(2,1)}), bf16[128,20,256]{2,1,0:T(8,128)(2,1)}) %all-gather.17.cloned.1.call-update) | async-done | bytes 1310736 | tf_op jit(solution)/shard_map/all_gather | solution.py:170
  881.4 3.1 reshape.465
  884.5 2.1 fusion.38
  886.7 2.3 fusion.67
  889.0 0.6 copy.63
  889.9 0.6 copy.64
  890.5 557.1 %reduce-scatter.2.cloned.1.call-done = f32[256,16]{0,1:T(8,128)} async-done(((f32[256,2048]{0,1:T(8,128)}), f32[256,16]{0,1:T(8,128)}) %reduce-scatter.2.cloned.1.call-update) | async-done | bytes 16400 | tf_op jit(solution)/shard_map/reduce_scatter | solution.py:178
  (187 shorter events, 17.6 us)
Async XLA Ops:
  7.2 23.4 %copy-start = (bf16[256,2048]{1,0:T(8,128)(2,1)S(1)}, bf16[256,2048]{1,0:T(8,128)(2,1)}, u32[]{:S(2)}) copy-start(bf16[256,2048]{1,0:T(8,128)(2,1)} %param.19) | copy-start | bytes 3145732
  7.2 223.4 %all-gather.11.cloned.1.call-start = ((), (), s32[]{:S(2)}) async-start(), calls=%async_computation.2 | async-start | bytes 1585152 | tf_op jit(solution)/shard_map/all_gather | solution.py:133
  7.9 439.4 %all-gather.13.cloned.1.call-start = ((), (), s32[]{:S(2)}) async-start(), calls=%async_computation.3 | async-start | bytes 1585152 | tf_op jit(solution)/shard_map/all_gather | solution.py:132
  8.7 786.5 %all-gather.15.cloned.1.call-start = ((), (), s32[]{:S(2)}) async-start(), calls=%async_computation.4 | async-start | bytes 1585152 | tf_op jit(solution)/shard_map/all_gather | solution.py:169
  9.4 872.0 %all-gather.17.cloned.1.call-start = ((), (), s32[]{:S(2)}) async-start(), calls=%async_computation.5 | async-start | bytes 1585152 | tf_op jit(solution)/shard_map/all_gather | solution.py:170
  11.0 4.2 copy-start.4
  29.4 2.3 copy-start.3
  29.4 3.2 copy-start.5
  31.6 1416.0 %reduce-scatter.2.cloned.1.call-start = ((), (), s32[]{:S(2)}) async-start(), calls=%async_computation.1 | async-start | bytes 2113536 | tf_op jit(solution)/shard_map/reduce_scatter | solution.py:178
  486.4 0.7 copy-start.1
  486.4 0.7 copy-start.2
Sparse Core Ops, SparseCore 0:
  10.2 220.3 all-gather.10
  232.7 214.5 all-gather.12
  449.5 214.7 all-gather.14
  666.8 214.5 all-gather.16
  884.6 562.9 reduce-scatter.1
where the time goes:
time: 1460 us; the launch traced here: 1450 us
  waiting for transfers between devices  1050 us (72%)
  blocking collectives  320 us (22%)
  local copies, waits for them, and re-layouts  43.7 us (3%)
  matrix products  17.6 us (1%)
    reduce_scatter x1, waiting for transfers between devices, on_device(): lax.psum_scatter(partial_value, 'seq', scatter_dimension=1, tiled=True)  557 us
    all_gather x1, waiting for transfers between devices, on_device(): lax.all_gather(attn_key, 'seq', axis=0, tiled=True)  213 us
    all_gather x1, waiting for transfers between devices, on_device(): lax.all_gather(attn_value, 'seq', axis=0, tiled=True)  198 us
    all_gather x1, blocking collectives, on_device(): lax.all_gather(log_total.T, 'seq', axis=0, tiled=True)  154 us
    all_gather x1, blocking collectives, on_device(): lax.all_gather(row_delta.T, 'seq', axis=0, tiled=True)  151 us
    all_gather x1, waiting for transfers between devices, on_device(): lax.all_gather(d_attn, 'seq', axis=0, tiled=True)  82.2 us
  transfers between devices with their start and end apart: 5, of which 4 were waited for; matrix products, arithmetic and copies ran while one was open for 5% of the time, Pallas kernels for 0%

commit v1 on v0

v1 whole, which is shorter than its diff:
```python
import jax
import jax.numpy as jnp
from jax import lax
from jax.experimental import pallas as pl
from jax.experimental.pallas import tpu as pltpu
from jax.sharding import Mesh
from jax.sharding import PartitionSpec as P

HS = 128
NZ = 8
NA = 16
TP = 4
SLOTS = 20
CAP2 = 16
PAD3 = 8
ROWS = CAP2 + PAD3
WIDTH = 2 * HS
SCALE = HS**-0.5
LOW = -1e30
F32 = jnp.float32
BF16 = jnp.bfloat16

NT = (((1,), (1,)), ((), ()))
NN = (((1,), (0,)), ((), ()))
TN = (((0,), (0,)), ((), ()))


def mm(left, right, dims):
    return lax.dot_general(left, right, dims, preferred_element_type=F32)


def split_rows(block):
    wide = block.astype(F32)
    count, _, width = wide.shape
    second = wide[:, :CAP2].reshape(count * CAP2, width).astype(BF16)
    third = wide[:, CAP2:].reshape(count * PAD3, width).astype(BF16)
    return second, third


def join_rows(second, third, count):
    width = second.shape[1]
    return jnp.concatenate(
        [second.reshape(count, CAP2, width), third.reshape(count, PAD3, width)], axis=1
    )


def allowed(counts_ref, which, slots, z_own, a_own):
    shape = (NZ * slots, NA * slots)
    key_row = lax.broadcasted_iota(jnp.int32, shape, 0)
    query_row = lax.broadcasted_iota(jnp.int32, shape, 1)
    key_z = key_row // slots
    key_slot = key_row % slots
    key_order = (key_z * NA + a_own) * slots + key_slot
    query_order = z_own * NA * slots + query_row
    limit = jnp.concatenate(
        [
            jnp.full((slots, NA * slots), counts_ref[z * NA + a_own, which], jnp.int32)
            for z in range(NZ)
        ],
        axis=0,
    )
    return (key_order <= query_order) & (key_slot < limit)


def project_kernel(place_ref, counts_ref, grad_ref, weight_ref, query_ref, key_ref, value_ref, qd_ref, kvg_ref):
    shard = place_ref[0] * NA + place_ref[1]
    slot = lax.broadcasted_iota(jnp.int32, (SLOTS, 512), 0)
    live = slot < jnp.where(slot < CAP2, counts_ref[shard, 0], CAP2 + counts_ref[shard, 1])
    total = jnp.zeros((SLOTS, WIDTH), F32)
    pieces = []
    for t in range(TP):
        piece = jnp.where(live, grad_ref[t].astype(F32), 0.0).astype(BF16)
        pieces.append(piece)
        total += mm(piece, weight_ref[:, t * 512 : (t + 1) * 512], NT)
    rest = jnp.zeros((ROWS - SLOTS, WIDTH), F32)

    def padded(block):
        return jnp.concatenate([block.astype(F32), rest], axis=0).astype(BF16)

    query = padded(query_ref[...])
    d_attn = padded(total.astype(BF16))
    key = padded(key_ref[...])
    value = padded(value_ref[...])
    for a in range(NA):
        qd_ref[a, :, :WIDTH] = query
        qd_ref[a, :, WIDTH:] = d_attn
    for z in range(NZ):
        kvg_ref[z, :, :WIDTH] = key
        kvg_ref[z, :, WIDTH : 2 * WIDTH] = value
        column = z * WIDTH
        kvg_ref[z, :, 2 * WIDTH :] = padded(pieces[column // 512][:, column % 512 : column % 512 + WIDTH])


def groups(kv, qd):
    kv_parts = split_rows(kv)
    qd_parts = split_rows(qd)
    return [(0, CAP2, kv_parts[0], qd_parts[0]), (1, PAD3, kv_parts[1], qd_parts[1])]


def stats_kernel(place_ref, counts_ref, kvg_ref, qd_ref, out_ref):
    z_own, a_own = place_ref[0], place_ref[1]
    rows = {}
    attended = {}
    for which, slots, kv, qd in groups(kvg_ref[:, :, : 2 * WIDTH], qd_ref[...]):
        mask = allowed(counts_ref, which, slots, z_own, a_own)
        for h in range(2):
            cols = slice(h * HS, (h + 1) * HS)
            cols2 = slice(WIDTH + h * HS, WIDTH + (h + 1) * HS)
            scores = jnp.where(mask, mm(kv[:, cols], qd[:, cols], NT) * SCALE, LOW)
            top = jnp.max(scores, axis=0, keepdims=True)
            weights = jnp.where(mask, jnp.exp(scores - top), 0.0)
            total = jnp.sum(weights, axis=0, keepdims=True)
            none = total == 0.0
            inverse = 1.0 / jnp.where(none, 1.0, total)
            weights = weights * inverse
            dprob = mm(kv[:, cols2], qd[:, cols2], NT)
            rows[which, h, 0] = jnp.where(none, LOW, top + jnp.log(jnp.where(none, 1.0, total)))
            rows[which, h, 1] = jnp.sum(weights * dprob, axis=0, keepdims=True)
            attended[which, h] = mm(weights.astype(BF16), kv[:, cols2], TN)
    for h in range(2):
        out_ref[:, :ROWS, h * HS : (h + 1) * HS] = join_rows(attended[0, h], attended[1, h], NA)
    stats = jnp.concatenate(
        [
            rows[0, 0, 0],
            rows[0, 1, 0],
            rows[0, 0, 1],
            rows[0, 1, 1],
            jnp.concatenate([rows[1, 0, 0], rows[1, 1, 0]], axis=1),
            jnp.concatenate([rows[1, 0, 1], rows[1, 1, 1]], axis=1),
            jnp.zeros((2, WIDTH), F32),
        ],
        axis=0,
    )
    for a in range(NA):
        out_ref[a, ROWS:, :] = stats


def grads_kernel(place_ref, counts_ref, kvg_ref, qd_ref, in_ref, out_ref, dq_ref, share2_ref, share3_ref):
    z_own, a_own = place_ref[0], place_ref[1]
    stat = {}
    for h in range(2):
        stat[0, h] = (in_ref[:, ROWS + h, :], in_ref[:, ROWS + 2 + h, :])
        cols = slice(h * HS, (h + 1) * HS)
        stat[1, h] = (in_ref[:, ROWS + 4, cols], in_ref[:, ROWS + 5, cols])
    log_total, delta = {}, {}
    for (which, h), (logs, deltas) in stat.items():
        top = jnp.max(logs, axis=0, keepdims=True)
        whole = top + jnp.log(jnp.sum(jnp.exp(logs - top), axis=0, keepdims=True))
        share = jnp.exp(logs - whole)
        log_total[which, h] = whole
        delta[which, h] = jnp.sum(share * deltas, axis=0, keepdims=True)
        if which == 0:
            share2_ref[h] = share.T
        else:
            share3_ref[h] = share.T
    own2 = pl.ds(pl.multiple_of(a_own * CAP2, CAP2), CAP2)
    own3 = pl.ds(pl.multiple_of(a_own * PAD3, PAD3), PAD3)
    attended = []
    for h in range(2):
        share = jnp.concatenate([share2_ref[h, own2, :], share3_ref[h, own3, :]], axis=0)
        cols = slice(h * HS, (h + 1) * HS)
        total = jnp.zeros((ROWS, HS), F32)
        for a in range(NA):
            total += share[:, a : a + 1] * in_ref[a, :ROWS, cols]
        attended.append(total.astype(BF16))
    attended = jnp.concatenate(attended, axis=1)

    d_query, d_key, d_value = {}, {}, {}
    for which, slots, kv, qd in groups(kvg_ref[:, :, : 2 * WIDTH], qd_ref[...]):
        mask = allowed(counts_ref, which, slots, z_own, a_own)
        for h in range(2):
            cols = slice(h * HS, (h + 1) * HS)
            cols2 = slice(WIDTH + h * HS, WIDTH + (h + 1) * HS)
            scores = mm(kv[:, cols], qd[:, cols], NT) * SCALE
            prob = jnp.where(mask, jnp.exp(jnp.where(mask, scores, LOW) - log_total[which, h]), 0.0)
            dprob = mm(kv[:, cols2], qd[:, cols2], NT)
            dscore = (prob * (dprob - delta[which, h])).astype(BF16)
            d_value[which, h] = mm(prob.astype(BF16), qd[:, cols2], NN)
            d_key[which, h] = mm(dscore, qd[:, cols], NN) * SCALE
            d_query[which, h] = mm(dscore, kv[:, cols], TN) * SCALE
    for h in range(2):
        cols = slice(h * HS, (h + 1) * HS)
        cols2 = slice(WIDTH + h * HS, WIDTH + (h + 1) * HS)
        out_ref[:, :, cols] = join_rows(d_key[0, h], d_key[1, h], NZ).astype(BF16)
        out_ref[:, :, cols2] = join_rows(d_value[0, h], d_value[1, h], NZ).astype(BF16)
        dq_ref[:, :, cols] = join_rows(d_query[0, h], d_query[1, h], NA)
    for z in range(NZ):
        out_ref[z, :, 2 * WIDTH :] = attended


def weight_kernel(in_ref, kvg_ref, dq_ref, dk_ref, dv_ref, out_ref):
    total = jnp.sum(in_ref[:, :, : 2 * WIDTH].astype(F32), axis=0)
    dk_ref[...] = total[:SLOTS, :WIDTH].astype(BF16)
    dv_ref[...] = total[:SLOTS, WIDTH:].astype(BF16)
    attended = in_ref[:, :, 2 * WIDTH :].astype(F32).reshape(NZ * ROWS, WIDTH).astype(BF16)
    columns = kvg_ref[:, :, 2 * WIDTH :].astype(F32).reshape(NZ * ROWS, WIDTH).astype(BF16)
    part = mm(columns, attended, TN)
    out_ref[:, :ROWS, :] = dq_ref[...]
    out_ref[:, ROWS:, :] = part.reshape(NA, WIDTH // NA, WIDTH)


def last_kernel(in_ref, dq_ref, dw_ref):
    total = jnp.sum(in_ref[...], axis=0)
    dq_ref[...] = total[:SLOTS].astype(BF16)
    dw_ref[...] = total[ROWS:]


def on_device(token_picks, live_counts, attn_query, attn_key, attn_value, out_grad, out_weight):
    del token_picks
    place = jnp.stack([lax.axis_index("z"), lax.axis_index("a")]).astype(jnp.int32)
    smem = pl.BlockSpec(memory_space=pltpu.SMEM)
    vmem = pl.BlockSpec(memory_space=pltpu.VMEM)

    def run(kernel, outs, args, scratch=(), scalars=2):
        return pl.pallas_call(
            kernel,
            out_shape=[jax.ShapeDtypeStruct(*o) for o in outs],
            in_specs=[smem] * scalars + [vmem] * (len(args) - scalars),
            out_specs=[vmem] * len(outs),
            scratch_shapes=list(scratch),
            compiler_params=pltpu.CompilerParams(vmem_limit_bytes=32 * 2**20),
        )(*args)

    grad = lax.all_gather(out_grad, "tp", axis=0, tiled=False)
    qd, kvg = run(
        project_kernel,
        [((NA, ROWS, 2 * WIDTH), BF16), ((NZ, ROWS, 3 * WIDTH), BF16)],
        (place, live_counts, grad, out_weight, attn_query, attn_key, attn_value),
    )
    kvg = lax.all_to_all(kvg, "z", 0, 0)
    qd = lax.all_to_all(qd, "a", 0, 0)
    (stats,) = run(stats_kernel, [((NA, ROWS + 8, WIDTH), F32)], (place, live_counts, kvg, qd))
    stats = lax.all_to_all(stats, "a", 0, 0)
    back, dq = run(
        grads_kernel,
        [((NZ, ROWS, 3 * WIDTH), BF16), ((NA, ROWS, WIDTH), F32)],
        (place, live_counts, kvg, qd, stats),
        [pltpu.VMEM((2, NA * CAP2, NA), F32), pltpu.VMEM((2, NA * PAD3, NA), F32)],
    )
    back = lax.all_to_all(back, "z", 0, 0)
    key_grad, value_grad, last = run(
        weight_kernel,
        [((SLOTS, WIDTH), BF16), ((SLOTS, WIDTH), BF16), ((NA, ROWS + WIDTH // NA, WIDTH), F32)],
        (back, kvg, dq),
        scalars=0,
    )
    last = lax.all_to_all(last, "a", 0, 0)
    query_grad, weight_grad = run(
        last_kernel, [((SLOTS, WIDTH), BF16), ((WIDTH // NA, WIDTH), F32)], (last,), scalars=0
    )
    return query_grad, key_grad, value_grad, weight_grad.T


def solution(mesh):
    grid = Mesh(mesh.devices.reshape(NZ, NA, TP), ("z", "a", "tp"))
    rows = P(("z", "a"), "tp")
    return jax.shard_map(
        on_device,
        mesh=grid,
        in_specs=(P(), P(), rows, rows, rows, rows, P("tp", None)),
        out_specs=(rows, rows, rows, P("tp", ("z", "a"))),
        check_vma=False,
    )
```

time: 1460 us -> 108 us (0.07)
  waiting for transfers between devices: 1050 us -> 0 us
  blocking collectives: 320 us -> 95.6 us
  local copies, waits for them, and re-layouts: 43.7 us -> 2.64 us
  matrix products: 17.6 us -> 0 us
    reduce_scatter x1 -> x0, waiting for transfers between devices: 557 us -> none  [on_device(): lax.psum_scatter(partial_value, 'seq', scatter_dimension=1, tiled=True)]
    all_gather x4 -> x0, waiting for transfers between devices: 494 us -> none  [the longest x1 213 us: on_device(): lax.all_gather(attn_key, 'seq', axis=0, tiled=True)]
    all_gather x3 -> x1, blocking collectives: 320 us -> 14.4 us  [on_device(): grad = lax.all_gather(out_grad, 'tp', axis=0, tiled=False)]
    all_to_all x0 -> x5, blocking collectives: none -> 81.2 us  [the longest x1 19.4 us: on_device(): kvg = lax.all_to_all(kvg, 'z', 0, 0)]
    dot_general x45 -> x0, matrix products: 17.6 us -> none  [the longest x17 6.07 us: masked_scores(): jnp.einsum('qhd,khd->hqk', query_part, key_part, preferred_element_type=j...]
    while x24 -> x0, local copies, waits for them, and re-layouts: 16.4 us -> none
  transfers between devices with their start and end apart: 5 -> 0, of which waited for: 4 -> 0; matrix products, arithmetic and copies ran while one was open for 5% -> 0% of each run, Pallas kernels for 0% -> 0%
where the time goes in v1:
time: 108 us; the launch traced here: 107 us
  blocking collectives  95.6 us (89%)
  Pallas kernels  8.51 us (8%)
  local copies, waits for them, and re-layouts  2.64 us (2%)
    all_to_all x1, blocking collectives, on_device(): kvg = lax.all_to_all(kvg, 'z', 0, 0)  19.4 us
    all_to_all x1, blocking collectives, on_device(): last = lax.all_to_all(last, 'a', 0, 0)  17.9 us
    all_to_all x1, blocking collectives, on_device(): qd = lax.all_to_all(qd, 'a', 0, 0)  17.4 us
    all_gather x1, blocking collectives, on_device(): grad = lax.all_gather(out_grad, 'tp', axis=0, tiled=False)  14.4 us
    all_to_all x1, blocking collectives, on_device(): stats = lax.all_to_all(stats, 'a', 0, 0)  13.5 us
    all_to_all x1, blocking collectives, on_device(): back = lax.all_to_all(back, 'z', 0, 0)  13 us
    pallas_call x5, Pallas kernels, run(): pl.pallas_call(kernel, out_shape=[jax.ShapeDtypeStruct(*o) for o in outs]...  8.51 us
    unnamed x13, local copies, waits for them, and re-layouts  2.64 us

profile of v1, /device:TPU:1, one launch (start us, length us, event | category | flops | bytes accessed | tf_op | source)
XLA Modules:
  0.0 107.5 jit_solution(15365113590840864506)
XLA Ops:
  0.6 0.0 copy-start.5
  0.6 0.7 copy-done.5
  1.3 0.0 copy-start.4
  1.3 0.1 copy.15.counts_ref
  1.4 0.6 copy-done.4
  2.1 0.0 copy-start.1
  2.1 0.0 copy-start.2
  2.1 0.0 copy-start.3
  2.1 14.4 %all-gather.1.grad_ref = bf16[4,20,512]{2,1,0:T(8,128)(2,1)S(1)} all-gather(bf16[1,20,512]{2,1,0:T(8,128)(2,1)S(1)} %bitcast.4), channel_id=2, replica_groups=mesh['z'=8,'a'=16,'tp'=4] {'tp'}, dimensions={0}, use_global_device_ids=true | all-gather | bytes 102400 | tf_op jit(solution)/shard_map/all_gather | solution.py:224
  16.4 0.1 pad_add_fusion.place_ref
  16.5 0.0 copy-done.1
  16.5 0.0 copy-done.2
  16.5 0.0 copy-done.3
  16.5 0.0 copy-start
  16.5 1.2 %copy-done = bf16[256,2048]{1,0:T(8,128)(2,1)S(1)} copy-done((bf16[256,2048]{1,0:T(8,128)(2,1)S(1)}, bf16[256,2048]{1,0:T(8,128)(2,1)}, u32[]{:S(2)}) %copy-start) | copy-done | bytes 1048600
  17.7 2.0 %shard_map.93 = (bf16[16,24,512]{2,1,0:T(8,128)(2,1)S(1)}, bf16[8,24,768]{2,1,0:T(8,128)(2,1)S(1)}) custom-call(s32[2]{0:T(128)S(1)} %pad_add_fusion.place_ref, s32[128,2]{1,0:T(8,128)S(1)} %copy.15.counts_ref, bf16[4,20,512]{2,1,0:T(8,128)(2,1)S(1)} %all-gather.1.grad_ref, bf16[256,2048]{1,0:T(8,128)(2,1)S(1)} %copy-done, bf16[20,256]{1,0:T(8,128)(2,1)S(1)} %copy-done.1, ...), custom_call_target="tpu_custom_call" | custom-call | tf_op jit(solution)/shard_map/pallas_call | solution.py:215
  19.8 19.4 %all_to_all.25.kvg_ref = bf16[8,24,768]{2,1,0:T(8,128)(2,1)S(1)} all-to-all(bf16[8,24,768]{2,1,0:T(8,128)(2,1)S(1)} %get-tuple-element.13), channel_id=1, replica_groups=mesh['z'=8,'a'=16,'tp'=4] {'z'}, dimensions={0} | all-to-all | bytes 589824 | tf_op jit(solution)/shard_map/all_to_all | solution.py:230
  39.2 17.4 %all_to_all.26.qd_ref = bf16[16,24,512]{2,1,0:T(8,128)(2,1)S(1)} all-to-all(bf16[16,24,512]{2,1,0:T(8,128)(2,1)S(1)} %get-tuple-element.14), channel_id=1, replica_groups=mesh['z'=8,'a'=16,'tp'=4] {'a'}, dimensions={0} | all-to-all | bytes 786432 | tf_op jit(solution)/shard_map/all_to_all | solution.py:231
  56.6 2.4 %shard_map.94 = f32[16,32,256]{2,1,0:T(8,128)S(1)} custom-call(s32[2]{0:T(128)S(1)} %pad_add_fusion.place_ref, s32[128,2]{1,0:T(8,128)S(1)} %copy.15.counts_ref, bf16[8,24,768]{2,1,0:T(8,128)(2,1)S(1)} %all_to_all.25.kvg_ref, bf16[16,24,512]{2,1,0:T(8,128)(2,1)S(1)} %all_to_all.26.qd_ref), custom_call_target="tpu_custom_call" | custom-call | tf_op jit(solution)/shard_map/pallas_call | solution.py:215
  59.0 13.5 %all_to_all.27.in_ref = f32[16,32,256]{2,1,0:T(8,128)S(1)} all-to-all(f32[16,32,256]{2,1,0:T(8,128)S(1)} %shard_map.94), channel_id=1, replica_groups=mesh['z'=8,'a'=16,'tp'=4] {'a'}, dimensions={0} | all-to-all | bytes 1048576 | tf_op jit(solution)/shard_map/all_to_all | solution.py:233
  72.5 2.7 %shard_map.95 = (bf16[8,24,768]{2,1,0:T(8,128)(2,1)S(1)}, f32[16,24,256]{2,1,0:T(8,128)S(1)}) custom-call(s32[2]{0:T(128)S(1)} %pad_add_fusion.place_ref, s32[128,2]{1,0:T(8,128)S(1)} %copy.15.counts_ref, bf16[8,24,768]{2,1,0:T(8,128)(2,1)S(1)} %all_to_all.25.kvg_ref, bf16[16,24,512]{2,1,0:T(8,128)(2,1)S(1)} %all_to_all.26.qd_ref, ...), custom_call_target="tpu_custom_call" | custom-call | tf_op jit(solution)/shard_map/pallas_call | solution.py:215
  75.2 13.0 %all_to_all.28.in_ref = bf16[8,24,768]{2,1,0:T(8,128)(2,1)S(1)} all-to-all(bf16[8,24,768]{2,1,0:T(8,128)(2,1)S(1)} %get-tuple-element.15), channel_id=1, replica_groups=mesh['z'=8,'a'=16,'tp'=4] {'z'}, dimensions={0} | all-to-all | bytes 589824 | tf_op jit(solution)/shard_map/all_to_all | solution.py:240
  88.2 0.8 shard_map.96
  88.9 17.9 %all_to_all.29.in_ref = f32[16,40,256]{2,1,0:T(8,128)S(1)} all-to-all(f32[16,40,256]{2,1,0:T(8,128)S(1)} %get-tuple-element.17), channel_id=1, replica_groups=mesh['z'=8,'a'=16,'tp'=4] {'a'}, dimensions={0} | all-to-all | bytes 1310720 | tf_op jit(solution)/shard_map/all_to_all | solution.py:247
  106.8 0.6 shard_map.97
Async XLA Ops:
  0.6 0.7 copy-start.5
  1.3 0.7 copy-start.4
  2.1 14.4 %copy-start.1 = (bf16[20,256]{1,0:T(8,128)(2,1)S(1)}, bf16[20,256]{1,0:T(8,128)(2,1)}, u32[]{:S(2)}) copy-start(bf16[20,256]{1,0:T(8,128)(2,1)} %query_ref.1) | copy-start | bytes 30724
  2.1 14.4 %copy-start.2 = (bf16[20,256]{1,0:T(8,128)(2,1)S(1)}, bf16[20,256]{1,0:T(8,128)(2,1)}, u32[]{:S(2)}) copy-start(bf16[20,256]{1,0:T(8,128)(2,1)} %key_ref.1) | copy-start | bytes 30724
  2.1 14.4 %copy-start.3 = (bf16[20,256]{1,0:T(8,128)(2,1)S(1)}, bf16[20,256]{1,0:T(8,128)(2,1)}, u32[]{:S(2)}) copy-start(bf16[20,256]{1,0:T(8,128)(2,1)} %value_ref.1) | copy-start | bytes 30724
  16.5 1.2 %copy-start = (bf16[256,2048]{1,0:T(8,128)(2,1)S(1)}, bf16[256,2048]{1,0:T(8,128)(2,1)}, u32[]{:S(2)}) copy-start(bf16[256,2048]{1,0:T(8,128)(2,1)} %weight_ref.1) | copy-start | bytes 3145732

commit v2 on v1

v2 whole, which is shorter than its diff:
```python
import jax
import jax.numpy as jnp
from jax import lax
from jax.experimental import pallas as pl
from jax.experimental.pallas import tpu as pltpu
from jax.sharding import Mesh
from jax.sharding import PartitionSpec as P

HS = 128
NZ, NY, NX, NC = 8, 2, 4, 2
FAR = ("z", "x")
NEAR = ("y", "c")
NF, NN_ = NZ * NX, NY * NC
TP = 4
SLOTS = 20
CAP2 = 16
CAP3 = 4
PAD3 = 8
ROWS = CAP2 + PAD3
WIDTH = 2 * HS
MODEL = 2048
COLS = MODEL // 128
QROWS = NN_ * ROWS
BACK = 2 * CAP2 + PAD3 + COLS
SCALE = HS**-0.5
LOW = -1e30
F32 = jnp.float32
BF16 = jnp.bfloat16

NT = (((1,), (1,)), ((), ()))
NN = (((1,), (0,)), ((), ()))
TN = (((0,), (0,)), ((), ()))


def mm(left, right, dims):
    return lax.dot_general(left, right, dims, preferred_element_type=F32)


def split_rows(block):
    wide = block.astype(F32)
    count, _, width = wide.shape
    second = wide[:, :CAP2].reshape(count * CAP2, width).astype(BF16)
    third = wide[:, CAP2:].reshape(count * PAD3, width).astype(BF16)
    return second, third


def by_head(rows):
    column = lax.broadcasted_iota(jnp.int32, rows.shape, 1)
    zero = jnp.zeros_like(rows)
    return jnp.concatenate(
        [jnp.where(column < HS, rows, zero), jnp.where(column < HS, zero, rows)], axis=0
    )


def head_blocks(both):
    count = both.shape[0] // 2
    column = lax.broadcasted_iota(jnp.int32, (count, WIDTH), 1)
    return jnp.where(column < HS, both[:count], both[count:])


def allowed(place_ref, counts_ref, which, slots):
    z, y, x, c = (place_ref[i] for i in range(4))
    shape = (NF * slots, 2 * NN_ * slots)
    key_row = lax.broadcasted_iota(jnp.int32, shape, 0)
    query_row = lax.broadcasted_iota(jnp.int32, shape, 1) % (NN_ * slots)
    key_far, key_slot = key_row // slots, key_row % slots
    key_shard = (((key_far // NX) * NY + y) * NX + key_far % NX) * NC + c
    near, query_slot = query_row // slots, query_row % slots
    query_shard = ((z * NY + near // NC) * NX + x) * NC + near % NC
    limit = jnp.concatenate(
        [
            jnp.full((slots, shape[1]), counts_ref[which, ((f // NX * NY + y) * NX + f % NX) * NC + c], jnp.int32)
            for f in range(NF)
        ],
        axis=0,
    )
    in_order = key_shard * slots + key_slot <= query_shard * slots + query_slot
    return in_order & (key_slot < limit)


def blocks(kv_ref, qd_ref):
    kv_parts = split_rows(kv_ref[...])
    qd_parts = split_rows(qd_ref[:, :, : 2 * WIDTH])
    found = []
    for which, slots in ((0, CAP2), (1, PAD3)):
        kv, qd = kv_parts[which], qd_parts[which]
        found.append(
            (which, slots, kv[:, :WIDTH], kv[:, WIDTH:], by_head(qd[:, :WIDTH]), by_head(qd[:, WIDTH:]))
        )
    return found


def padded(block):
    rest = jnp.zeros((ROWS - SLOTS, block.shape[1]), F32)
    return jnp.concatenate([block.astype(F32), rest], axis=0).astype(BF16)


def project_kernel(place_ref, counts_ref, grad_ref, weight_ref, query_ref, out_ref):
    z, y, x, c = (place_ref[i] for i in range(4))
    shard = ((z * NY + y) * NX + x) * NC + c
    slot = lax.broadcasted_iota(jnp.int32, (SLOTS, 512), 0)
    live = slot < jnp.where(slot < CAP2, counts_ref[0, shard], CAP2 + counts_ref[1, shard])
    total = jnp.zeros((SLOTS, WIDTH), F32)
    for t in range(TP):
        piece = jnp.where(live, grad_ref[t].astype(F32), 0.0).astype(BF16)
        total += mm(piece, weight_ref[:, t * 512 : (t + 1) * 512], NT)
        out_ref[:, 2 * WIDTH + t * 512 : 2 * WIDTH + (t + 1) * 512] = padded(piece)
    out_ref[:, :WIDTH] = padded(query_ref[...])
    out_ref[:, WIDTH : 2 * WIDTH] = padded(total.astype(BF16))


def stats_kernel(place_ref, counts_ref, kv_ref, qd_ref, out_ref):
    start = 0
    stats = []
    for which, slots, key, value, query, d_attn in blocks(kv_ref, qd_ref):
        mask = allowed(place_ref, counts_ref, which, slots)
        scores = jnp.where(mask, mm(key, query, NT) * SCALE, LOW)
        top = jnp.max(scores, axis=0, keepdims=True)
        weights = jnp.where(mask, jnp.exp(scores - top), 0.0)
        total = jnp.sum(weights, axis=0, keepdims=True)
        none = total == 0.0
        weights = weights * (1.0 / jnp.where(none, 1.0, total))
        logs = jnp.where(none, LOW, top + jnp.log(jnp.where(none, 1.0, total)))
        delta = jnp.sum(weights * mm(value, d_attn, NT), axis=0, keepdims=True)
        attended = head_blocks(mm(weights.astype(BF16), value, TN))
        out_ref[start : start + NN_ * slots] = attended
        start += NN_ * slots
        rest = jnp.zeros((1, WIDTH - logs.shape[1]), F32)
        stats += [jnp.concatenate([logs, rest], axis=1), jnp.concatenate([delta, rest], axis=1)]
    out_ref[start:] = jnp.concatenate(stats + [jnp.zeros((8 - len(stats), WIDTH), F32)], axis=0)


def grads_kernel(place_ref, counts_ref, kv_ref, qd_ref, in_ref, out_ref, dq_ref):
    y, c = place_ref[1], place_ref[3]
    attended = []
    d_key, d_value = [], []
    start = 0
    for which, slots, key, value, query, d_attn in blocks(kv_ref, qd_ref):
        count = NN_ * slots
        logs = in_ref[:, QROWS + 2 * which, : 2 * count]
        deltas = in_ref[:, QROWS + 2 * which + 1, : 2 * count]
        top = jnp.max(logs, axis=0, keepdims=True)
        log_total = top + jnp.log(jnp.sum(jnp.exp(logs - top), axis=0, keepdims=True))
        share = jnp.exp(logs - log_total)
        delta = jnp.sum(share * deltas, axis=0, keepdims=True)
        share_down = jnp.concatenate([share, jnp.zeros((8 - NN_, 2 * count), F32)], axis=0).T
        column = lax.broadcasted_iota(jnp.int32, (count, WIDTH), 1)
        total = jnp.zeros((count, WIDTH), F32)
        for n in range(NN_):
            own = jnp.where(column < HS, share_down[:count, n : n + 1], share_down[count:, n : n + 1])
            total += own * in_ref[n, start : start + count]
        attended.append(total)

        mask = allowed(place_ref, counts_ref, which, slots)
        scores = jnp.where(mask, mm(key, query, NT) * SCALE, LOW)
        prob = jnp.where(mask, jnp.exp(scores - log_total), 0.0)
        dscore = (prob * (mm(value, d_attn, NT) - delta)).astype(BF16)
        d_value.append(mm(prob.astype(BF16), d_attn, NN).reshape(NF, slots, WIDTH))
        d_key.append((mm(dscore, query, NN) * SCALE).reshape(NF, slots, WIDTH))
        dq_ref[start : start + count] = head_blocks(mm(dscore, key, TN)) * SCALE
        start += count
    out_ref[:, :CAP2] = d_key[0].astype(BF16)
    out_ref[:, CAP2 : 2 * CAP2] = d_value[0].astype(BF16)
    attended = jnp.concatenate(attended, axis=0).astype(BF16)
    parts = []
    for z in range(NZ):
        column = pl.multiple_of(2 * WIDTH + (z * NY + y) * HS, HS)
        second, third = split_rows(qd_ref[:, :, pl.ds(column, HS)])
        grad = jnp.concatenate([second, third], axis=0)
        parts.append(mm(grad, attended, TN).reshape(NX, NC, COLS, WIDTH))
    parts = jnp.concatenate(parts, axis=0)
    own = jnp.where(c == 0, parts[:, 0], parts[:, 1])
    third = jnp.concatenate([d_key[1][:, :CAP3], d_value[1][:, :CAP3]], axis=1)
    out_ref[:, 2 * CAP2 :] = jnp.concatenate([third, own], axis=1).astype(BF16)


def query_kernel(place_ref, in_ref, dq_ref):
    near = place_ref[1] * NC + place_ref[3]
    second = pl.ds(pl.multiple_of(near * CAP2, CAP2), CAP2)
    third = pl.ds(pl.multiple_of(NN_ * CAP2 + near * PAD3, PAD3), PAD3)
    total = jnp.concatenate(
        [jnp.sum(in_ref[:, second, :], axis=0), jnp.sum(in_ref[:, third, :], axis=0)[:CAP3]], axis=0
    )
    dq_ref[...] = total.astype(BF16)


def last_kernel(in_ref, dk_ref, dv_ref, dw_ref):
    total = jnp.sum(in_ref[...].astype(F32), axis=0)
    third = 2 * CAP2
    dk_ref[...] = jnp.concatenate([total[:CAP2], total[third : third + CAP3]], axis=0).astype(BF16)
    dv_ref[...] = jnp.concatenate(
        [total[CAP2 : 2 * CAP2], total[third + CAP3 : third + 2 * CAP3]], axis=0
    ).astype(BF16)
    dw_ref[...] = total[third + PAD3 :]


def on_device(token_picks, live_counts, attn_query, attn_key, attn_value, out_grad, out_weight):
    del token_picks
    place = jnp.stack([lax.axis_index(a) for a in ("z", "y", "x", "c")]).astype(jnp.int32)
    smem = pl.BlockSpec(memory_space=pltpu.SMEM)
    vmem = pl.BlockSpec(memory_space=pltpu.VMEM)

    def run(kernel, outs, args, scalars):
        return pl.pallas_call(
            kernel,
            out_shape=[jax.ShapeDtypeStruct(*o) for o in outs],
            in_specs=[smem] * scalars + [vmem] * (len(args) - scalars),
            out_specs=[vmem] * len(outs),
            compiler_params=pltpu.CompilerParams(vmem_limit_bytes=32 * 2**20),
        )(*args)

    live_counts = live_counts.T
    kv = jnp.pad(jnp.concatenate([attn_key, attn_value], axis=1), ((0, ROWS - SLOTS), (0, 0)))
    kv = jnp.broadcast_to(kv[None], (NF, ROWS, 2 * WIDTH))
    kv = lax.all_to_all(kv, FAR, 0, 0)
    grad = lax.all_gather(out_grad, "tp", axis=0, tiled=False)
    (qd,) = run(
        project_kernel,
        [((ROWS, 2 * WIDTH + MODEL), BF16)],
        (place, live_counts, grad, out_weight, attn_query),
        2,
    )
    qd = lax.all_gather(qd, NEAR, axis=0, tiled=False)
    (stats,) = run(stats_kernel, [((QROWS + 8, WIDTH), F32)], (place, live_counts, kv, qd), 2)
    stats = lax.all_gather(stats, NEAR, axis=0, tiled=False)
    back, dq = run(
        grads_kernel,
        [((NF, BACK, WIDTH), BF16), ((QROWS, WIDTH), F32)],
        (place, live_counts, kv, qd, stats),
        2,
    )
    back = lax.all_to_all(back, FAR, 0, 0)
    dq = lax.all_gather(dq, NEAR, axis=0, tiled=False)
    (query_grad,) = run(query_kernel, [((SLOTS, WIDTH), BF16)], (place, dq), 1)
    key_grad, value_grad, weight_grad = run(
        last_kernel,
        [((SLOTS, WIDTH), BF16), ((SLOTS, WIDTH), BF16), ((COLS, WIDTH), F32)],
        (back,),
        0,
    )
    return query_grad, key_grad, value_grad, weight_grad.T


def solution(mesh):
    grid = Mesh(mesh.devices.reshape(NZ, NY, NX, NC, TP), ("z", "y", "x", "c", "tp"))
    seq = ("z", "y", "x", "c")
    rows = P(seq, "tp")
    return jax.shard_map(
        on_device,
        mesh=grid,
        in_specs=(P(), P(), rows, rows, rows, rows, P("tp", None)),
        out_specs=(rows, rows, rows, P("tp", seq)),
        check_vma=False,
    )
```

time: 108 us -> 88.8 us (0.82)
  blocking collectives: 95.6 us -> 37 us
  starting transfers between devices: 0 us -> 23.3 us
  waiting for transfers between devices: 0 us -> 16.6 us
  Pallas kernels: 8.51 us -> 6.93 us
    all_to_all x5 -> x0, blocking collectives: 81.2 us -> none  [the longest x1 19.4 us: on_device(): kvg = lax.all_to_all(kvg, 'z', 0, 0)]
    all_to_all x0 -> x2, starting transfers between devices: none -> 23.3 us  [the longest x1 13.8 us: on_device(): kv = lax.all_to_all(kv, FAR, 0, 0)]
    all_gather x0 -> x3, blocking collectives: none -> 22.8 us  [the longest x1 9.51 us: on_device(): qd = lax.all_gather(qd, NEAR, axis=0, tiled=False)]
    all_to_all x0 -> x2, waiting for transfers between devices: none -> 16.6 us  [the longest x1 16.6 us: on_device(): back = lax.all_to_all(back, FAR, 0, 0)]
    pallas_call x5, Pallas kernels: 8.51 us -> 6.93 us  [run(): pl.pallas_call(kernel, out_shape=[jax.ShapeDtypeStruct(*o) for o in outs]...]
    unnamed x13 -> x8, local copies, waits for them, and re-layouts: 2.64 us -> 1.41 us
  transfers between devices with their start and end apart: 0 -> 2, of which waited for: 0 -> 1; matrix products, arithmetic and copies ran while one was open for 0% -> 0% of each run, Pallas kernels for 0% -> 2%
where the time goes in v2:
time: 88.8 us; the launch traced here: 87.7 us
  blocking collectives  37 us (42%)
  starting transfers between devices  23.3 us (26%)
  waiting for transfers between devices  16.6 us (19%)
  Pallas kernels  6.93 us (8%)
  local copies, waits for them, and re-layouts  2.34 us (3%)
    all_to_all x1, waiting for transfers between devices, on_device(): back = lax.all_to_all(back, FAR, 0, 0)  16.6 us
    all_gather x1, blocking collectives, on_device(): grad = lax.all_gather(out_grad, 'tp', axis=0, tiled=False)  14.1 us
    all_to_all x1, starting transfers between devices, on_device(): kv = lax.all_to_all(kv, FAR, 0, 0)  13.8 us
    all_gather x1, blocking collectives, on_device(): qd = lax.all_gather(qd, NEAR, axis=0, tiled=False)  9.51 us
    all_to_all x1, starting transfers between devices, on_device(): back = lax.all_to_all(back, FAR, 0, 0)  9.49 us
    pallas_call x5, Pallas kernels, run(): pl.pallas_call(kernel, out_shape=[jax.ShapeDtypeStruct(*o) for o in outs]...  6.93 us
    all_gather x1, blocking collectives, on_device(): stats = lax.all_gather(stats, NEAR, axis=0, tiled=False)  6.75 us
    all_gather x1, blocking collectives, on_device(): dq = lax.all_gather(dq, NEAR, axis=0, tiled=False)  6.58 us
  transfers between devices with their start and end apart: 2, of which 1 were waited for; matrix products, arithmetic and copies ran while one was open for 0% of the time, Pallas kernels for 2%

profile of v2, /device:TPU:1, one launch (start us, length us, event | category | flops | bytes accessed | tf_op | source)
XLA Modules:
  0.0 87.7 jit_solution(9693714938805637816)
XLA Ops:
  0.6 0.7 fusion.2
  1.4 0.9 %broadcast_in_dim.2 = bf16[32,24,512]{2,1,0:T(8,128)(2,1)} broadcast(bf16[24,512]{1,0:T(8,128)(2,1)S(1)} %fusion.2), dimensions={1,2} | broadcast | bytes 811008 | tf_op jit(solution)/shard_map/broadcast_in_dim | solution.py:214
  2.3 0.0 copy-start
  2.3 13.8 %all-to-all-start = ((bf16[32,24,512]{2,1,0:T(8,128)(2,1)}), bf16[32,24,512]{2,1,0:T(8,128)(2,1)S(1)}, u32[]{:S(2)}, u32[]{:S(2)}) async-start(bf16[32,24,512]{2,1,0:T(8,128)(2,1)} %broadcast_in_dim.2), calls=%async_computation | async-start | bytes 1572864 | tf_op jit(solution)/shard_map/all_to_all | solution.py:215
  16.2 0.0 copy-start.3
  16.2 0.7 copy-done.3
  16.9 0.0 copy-start.1
  16.9 14.1 %all-gather.4.grad_ref = bf16[4,20,512]{2,1,0:T(8,128)(2,1)S(1)} all-gather(bf16[1,20,512]{2,1,0:T(8,128)(2,1)S(1)} %bitcast.17), channel_id=2, replica_groups=mesh['z'=8,'y'=2,'x'=4,'c'=2,'tp'=4] {'tp'}, dimensions={0}, use_global_device_ids=true | all-gather | bytes 102400 | tf_op jit(solution)/shard_map/all_gather | solution.py:216
  31.0 0.1 pad_add_fusion.place_ref
  31.1 0.0 copy-start.2
  31.1 0.0 copy-done
  31.1 0.0 copy-done.1
  31.1 0.7 copy-done.2
  31.8 0.9 %shard_map.93 = bf16[24,2560]{1,0:T(8,128)(2,1)S(1)} custom-call(s32[4]{0:T(128)S(1)} %pad_add_fusion.place_ref, s32[2,128]{1,0:T(2,128)S(1)} %bitcast.14, bf16[4,20,512]{2,1,0:T(8,128)(2,1)S(1)} %all-gather.4.grad_ref, bf16[256,2048]{1,0:T(8,128)(2,1)S(1)} %copy-done, bf16[20,256]{1,0:T(8,128)(2,1)S(1)} %copy-done.1), custom_call_target="tpu_custom_call" | custom-call | tf_op jit(solution)/shard_map/pallas_call | solution.py:204
  32.7 9.5 %all-gather.1 = bf16[96,2560]{1,0:T(8,128)(2,1)S(1)} all-gather(bf16[24,2560]{1,0:T(8,128)(2,1)S(1)} %shard_map.93), channel_id=3, replica_groups=mesh['z'=8,'y'=2,'x'=4,'c'=2,'tp'=4] {'y','c'}, dimensions={0}, use_global_device_ids=true | all-gather | bytes 614400 | tf_op jit(solution)/shard_map/all_gather | solution.py:223
  42.2 0.0 all-to-all-done.kv_ref
  42.2 1.5 %shard_map.94 = f32[104,256]{1,0:T(8,128)S(1)} custom-call(s32[4]{0:T(128)S(1)} %pad_add_fusion.place_ref, s32[2,128]{1,0:T(2,128)S(1)} %bitcast.15, bf16[32,24,512]{2,1,0:T(8,128)(2,1)S(1)} %all-to-all-done.kv_ref, bf16[4,24,2560]{2,1,0:T(8,128)(2,1)S(1)} %bitcast.10), custom_call_target="tpu_custom_call" | custom-call | tf_op jit(solution)/shard_map/pallas_call | solution.py:204
  43.8 6.8 %all-gather.2 = f32[416,256]{1,0:T(8,128)S(1)} all-gather(f32[104,256]{1,0:T(8,128)S(1)} %shard_map.94), channel_id=4, replica_groups=mesh['z'=8,'y'=2,'x'=4,'c'=2,'tp'=4] {'y','c'}, dimensions={0}, use_global_device_ids=true | all-gather | bytes 532480 | tf_op jit(solution)/shard_map/all_gather | solution.py:225
  50.5 2.6 %shard_map.95 = (bf16[32,56,256]{2,1,0:T(8,128)(2,1)}, f32[96,256]{1,0:T(8,128)S(1)}) custom-call(s32[4]{0:T(128)S(1)} %pad_add_fusion.place_ref, s32[2,128]{1,0:T(2,128)S(1)} %bitcast.16, bf16[32,24,512]{2,1,0:T(8,128)(2,1)S(1)} %all-to-all-done.kv_ref, bf16[4,24,2560]{2,1,0:T(8,128)(2,1)S(1)} %bitcast.11, f32[4,104,256]{2,1,0:T(8,128)S(1)} %bitcast.12), custom_call_target="tpu_custom_call" | custom-call | tf_op jit(solution)/shard_map/pallas_call | solution.py:204
  53.1 9.5 %all-to-all-start.1 = ((bf16[32,56,256]{2,1,0:T(8,128)(2,1)}), bf16[32,56,256]{2,1,0:T(8,128)(2,1)S(1)}, u32[]{:S(2)}, u32[]{:S(2)}) async-start(bf16[32,56,256]{2,1,0:T(8,128)(2,1)} %get-tuple-element.10), calls=%async_computation.1 | async-start | bytes 1835008 | tf_op jit(solution)/shard_map/all_to_all | solution.py:232
  62.6 6.6 %all-gather.3 = f32[384,256]{1,0:T(8,128)S(1)} all-gather(f32[96,256]{1,0:T(8,128)S(1)} %get-tuple-element.9), channel_id=5, replica_groups=mesh['z'=8,'y'=2,'x'=4,'c'=2,'tp'=4] {'y','c'}, dimensions={0}, use_global_device_ids=true | all-gather | bytes 491520 | tf_op jit(solution)/shard_map/all_gather | solution.py:233
  69.2 1.2 %shard_map.96 = bf16[20,256]{1,0:T(8,128)(2,1)} custom-call(s32[4]{0:T(128)S(1)} %pad_add_fusion.place_ref, f32[4,96,256]{2,1,0:T(8,128)S(1)} %bitcast.13), custom_call_target="tpu_custom_call" | custom-call | tf_op jit(solution)/shard_map/pallas_call | solution.py:204
  70.3 16.6 %all-to-all-done.1.in_ref = bf16[32,56,256]{2,1,0:T(8,128)(2,1)S(1)} async-done(((bf16[32,56,256]{2,1,0:T(8,128)(2,1)}), bf16[32,56,256]{2,1,0:T(8,128)(2,1)S(1)}, u32[]{:S(2)}, u32[]{:S(2)}) %all-to-all-start.1) | async-done | bytes 917536 | tf_op jit(solution)/shard_map/all_to_all | solution.py:232
  86.9 0.7 shard_map.97
Async XLA Ops:
  2.3 28.8 %copy-start = (bf16[256,2048]{1,0:T(8,128)(2,1)S(1)}, bf16[256,2048]{1,0:T(8,128)(2,1)}, u32[]{:S(2)}) copy-start(bf16[256,2048]{1,0:T(8,128)(2,1)} %weight_ref.1) | copy-start | bytes 3145732
  2.3 39.9 %all-to-all-start = ((bf16[32,24,512]{2,1,0:T(8,128)(2,1)}), bf16[32,24,512]{2,1,0:T(8,128)(2,1)S(1)}, u32[]{:S(2)}, u32[]{:S(2)}) async-start(bf16[32,24,512]{2,1,0:T(8,128)(2,1)} %broadcast_in_dim.2), calls=%async_computation | async-start | bytes 1572864 | tf_op jit(solution)/shard_map/all_to_all | solution.py:215
  16.2 0.7 copy-start.3
  16.9 14.2 %copy-start.1 = (bf16[20,256]{1,0:T(8,128)(2,1)S(1)}, bf16[20,256]{1,0:T(8,128)(2,1)}, u32[]{:S(2)}) copy-start(bf16[20,256]{1,0:T(8,128)(2,1)} %query_ref.1) | copy-start | bytes 30724
  31.1 0.7 copy-start.2
  53.1 33.9 %all-to-all-start.1 = ((bf16[32,56,256]{2,1,0:T(8,128)(2,1)}), bf16[32,56,256]{2,1,0:T(8,128)(2,1)S(1)}, u32[]{:S(2)}, u32[]{:S(2)}) async-start(bf16[32,56,256]{2,1,0:T(8,128)(2,1)} %get-tuple-element.10), calls=%async_computation.1 | async-start | bytes 1835008 | tf_op jit(solution)/shard_map/all_to_all | solution.py:232

commit v3 on v2

v3 whole, which is shorter than its diff:
```python
import jax
import jax.numpy as jnp
from jax import lax
from jax.experimental import pallas as pl
from jax.experimental.pallas import tpu as pltpu
from jax.sharding import Mesh
from jax.sharding import PartitionSpec as P

HS = 128
NZ, NY, NX, NC = 8, 2, 4, 2
FAR = ("z", "x")
NEAR = ("y", "c")
NF, NEARS = NZ * NX, NY * NC
TP = 4
SLOTS = 20
CAP2 = 16
CAP3 = 4
PAD3 = 8
ROWS = CAP2 + PAD3
WIDTH = 2 * HS
MODEL = 2048
COLS = MODEL // 128
QROWS = NEARS * ROWS
BACK = 2 * CAP2 + PAD3 + COLS
SCALE = HS**-0.5
LOW = -1e30
F32 = jnp.float32
BF16 = jnp.bfloat16

NT = (((1,), (1,)), ((), ()))
NN = (((1,), (0,)), ((), ()))
TN = (((0,), (0,)), ((), ()))


def mm(left, right, dims):
    return lax.dot_general(left, right, dims, preferred_element_type=F32)


def split_rows(block):
    wide = block.astype(F32)
    count, _, width = wide.shape
    second = wide[:, :CAP2].reshape(count * CAP2, width).astype(BF16)
    third = wide[:, CAP2:].reshape(count * PAD3, width).astype(BF16)
    return second, third


def by_head(rows):
    column = lax.broadcasted_iota(jnp.int32, rows.shape, 1)
    zero = jnp.zeros_like(rows)
    return jnp.concatenate(
        [jnp.where(column < HS, rows, zero), jnp.where(column < HS, zero, rows)], axis=0
    )


def head_blocks(both):
    count = both.shape[0] // 2
    column = lax.broadcasted_iota(jnp.int32, (count, WIDTH), 1)
    return jnp.where(column < HS, both[:count], both[count:])


def shard_of(z, y, x, c):
    return ((z * NY + y) * NX + x) * NC + c


def place():
    return tuple(lax.axis_index(axis) for axis in ("z", "y", "x", "c"))


def allowed(limit_ref, which, slots):
    z, y, x, c = place()
    shape = (NF * slots, 2 * NEARS * slots)
    key_row = lax.broadcasted_iota(jnp.int32, shape, 0)
    query_row = lax.broadcasted_iota(jnp.int32, shape, 1) % (NEARS * slots)
    key_far, key_slot = key_row // slots, key_row % slots
    key_shard = shard_of(key_far // NX, y, key_far % NX, c)
    near, query_slot = query_row // slots, query_row % slots
    query_shard = shard_of(z, near // NC, x, near % NC)
    limit = limit_ref[which * NF : (which + 1) * NF, : shape[1]]
    limit = jnp.broadcast_to(limit[:, None, :], (NF, slots, shape[1])).reshape(shape)
    in_order = key_shard * slots + key_slot <= query_shard * slots + query_slot
    return in_order & (key_slot < limit)


def blocks(kv_ref, qd_ref):
    kv = kv_ref[...].astype(F32)
    third = kv[:, 2 * CAP2 :]
    shifted = jnp.concatenate([third[:, CAP3:], third[:, :CAP3]], axis=1)
    pairs = ((kv[:, :CAP2], kv[:, CAP2 : 2 * CAP2]), (third, shifted))
    qd_parts = split_rows(qd_ref[:, :, : 2 * WIDTH])
    found = []
    for which, slots in ((0, CAP2), (1, PAD3)):
        key, value = (part.reshape(NF * slots, WIDTH).astype(BF16) for part in pairs[which])
        qd = qd_parts[which]
        found.append((which, slots, key, value, by_head(qd[:, :WIDTH]), by_head(qd[:, WIDTH:])))
    return found


def padded(block):
    rest = jnp.zeros((ROWS - SLOTS, block.shape[1]), F32)
    return jnp.concatenate([block.astype(F32), rest], axis=0).astype(BF16)


def start_kernel(
    counts_any, key_any, value_any, grad_any, kv_any, grad_ref, limit_ref, counts, key, value, grad, block, sems, out_sems
):
    moves = [
        pltpu.make_async_copy(source, target, sems.at[i])
        for i, (source, target) in enumerate(
            ((key_any, key), (value_any, value), (counts_any, counts), (grad_any, grad))
        )
    ]
    for move in moves:
        move.start()
    moves[0].wait()
    moves[1].wait()
    keys, values = key[...].astype(F32), value[...].astype(F32)
    block[...] = jnp.concatenate(
        [keys[:CAP2], values[:CAP2], keys[CAP2:], values[CAP2:]], axis=0
    ).astype(BF16)
    sends = [pltpu.make_async_copy(block, kv_any.at[f], out_sems.at[f]) for f in range(NF)]
    for send in sends:
        send.start()
    moves[2].wait()
    moves[3].wait()
    z, y, x, c = place()
    shard = shard_of(z, y, x, c)
    slot = lax.broadcasted_iota(jnp.int32, (SLOTS, 512), 0)
    live = slot < jnp.where(slot < CAP2, counts[0, shard], CAP2 + counts[1, shard])
    grad_ref[...] = jnp.where(live, grad[...].astype(F32), 0.0).astype(BF16)
    for which in range(2):
        for f in range(NF):
            limit = counts[which, shard_of(f // NX, y, f % NX, c)]
            limit_ref[which * NF + f : which * NF + f + 1, :] = jnp.full((1, HS), limit, jnp.int32)
    for send in sends:
        send.wait()


def project_kernel(grad_ref, weight_ref, query_ref, out_ref):
    total = jnp.zeros((SLOTS, WIDTH), F32)
    for t in range(TP):
        piece = grad_ref[t]
        total += mm(piece, weight_ref[:, t * 512 : (t + 1) * 512], NT)
        out_ref[:, 2 * WIDTH + t * 512 : 2 * WIDTH + (t + 1) * 512] = padded(piece)
    out_ref[:, :WIDTH] = padded(query_ref[...])
    out_ref[:, WIDTH : 2 * WIDTH] = padded(total.astype(BF16))


def stats_kernel(limit_ref, kv_ref, qd_ref, out_ref, *kept):
    start = 0
    stats = []
    for which, slots, key, value, query, d_attn in blocks(kv_ref, qd_ref):
        mask = allowed(limit_ref, which, slots)
        scores = jnp.where(mask, mm(key, query, NT) * SCALE, LOW)
        dprob = mm(value, d_attn, NT)
        kept[2 * which][...] = scores
        kept[2 * which + 1][...] = dprob
        top = jnp.max(scores, axis=0, keepdims=True)
        weights = jnp.where(mask, jnp.exp(scores - top), 0.0)
        total = jnp.sum(weights, axis=0, keepdims=True)
        none = total == 0.0
        weights = weights * (1.0 / jnp.where(none, 1.0, total))
        logs = jnp.where(none, LOW, top + jnp.log(jnp.where(none, 1.0, total)))
        delta = jnp.sum(weights * dprob, axis=0, keepdims=True)
        attended = head_blocks(mm(weights.astype(BF16), value, TN))
        out_ref[start : start + NEARS * slots] = attended
        start += NEARS * slots
        rest = jnp.zeros((1, WIDTH - logs.shape[1]), F32)
        stats += [jnp.concatenate([logs, rest], axis=1), jnp.concatenate([delta, rest], axis=1)]
    out_ref[start:] = jnp.concatenate(stats + [jnp.zeros((8 - len(stats), WIDTH), F32)], axis=0)


def grads_kernel(kv_ref, qd_ref, in_ref, *refs):
    kept, (out_ref, dq_ref) = refs[:4], refs[4:]
    _, y, _, c = place()
    attended = []
    d_key, d_value = [], []
    start = 0
    for which, slots, key, _, query, d_attn in blocks(kv_ref, qd_ref):
        count = NEARS * slots
        logs = in_ref[:, QROWS + 2 * which, : 2 * count]
        deltas = in_ref[:, QROWS + 2 * which + 1, : 2 * count]
        top = jnp.max(logs, axis=0, keepdims=True)
        log_total = top + jnp.log(jnp.sum(jnp.exp(logs - top), axis=0, keepdims=True))
        share = jnp.exp(logs - log_total)
        delta = jnp.sum(share * deltas, axis=0, keepdims=True)
        share_down = jnp.concatenate([share, jnp.zeros((8 - NEARS, 2 * count), F32)], axis=0).T
        column = lax.broadcasted_iota(jnp.int32, (count, WIDTH), 1)
        total = jnp.zeros((count, WIDTH), F32)
        for n in range(NEARS):
            own = jnp.where(column < HS, share_down[:count, n : n + 1], share_down[count:, n : n + 1])
            total += own * in_ref[n, start : start + count]
        attended.append(total)

        prob = jnp.exp(kept[2 * which][...] - log_total)
        dscore = (prob * (kept[2 * which + 1][...] - delta)).astype(BF16)
        d_value.append(mm(prob.astype(BF16), d_attn, NN).reshape(NF, slots, WIDTH))
        d_key.append((mm(dscore, query, NN) * SCALE).reshape(NF, slots, WIDTH))
        dq_ref[start : start + count] = head_blocks(mm(dscore, key, TN)) * SCALE
        start += count
    out_ref[:, :CAP2] = d_key[0].astype(BF16)
    out_ref[:, CAP2 : 2 * CAP2] = d_value[0].astype(BF16)
    attended = jnp.concatenate(attended, axis=0).astype(BF16)
    parts = []
    for z in range(NZ):
        column = pl.multiple_of(2 * WIDTH + (z * NY + y) * HS, HS)
        second, third = split_rows(qd_ref[:, :, pl.ds(column, HS)])
        grad = jnp.concatenate([second, third], axis=0)
        parts.append(mm(grad, attended, TN).reshape(NX, NC, COLS, WIDTH))
    parts = jnp.concatenate(parts, axis=0)
    own = jnp.where(c == 0, parts[:, 0], parts[:, 1])
    third = jnp.concatenate([d_key[1][:, :CAP3], d_value[1][:, :CAP3]], axis=1)
    out_ref[:, 2 * CAP2 :] = jnp.concatenate([third, own], axis=1).astype(BF16)


def query_kernel(in_ref, dq_ref):
    _, y, _, c = place()
    near = y * NC + c
    second = pl.ds(pl.multiple_of(near * CAP2, CAP2), CAP2)
    third = pl.ds(pl.multiple_of(NEARS * CAP2 + near * PAD3, PAD3), PAD3)
    total = jnp.concatenate(
        [jnp.sum(in_ref[:, second, :], axis=0), jnp.sum(in_ref[:, third, :], axis=0)[:CAP3]], axis=0
    )
    dq_ref[...] = total.astype(BF16)


def last_kernel(in_ref, dk_ref, dv_ref, dw_ref):
    total = jnp.sum(in_ref[...].astype(F32), axis=0)
    third = 2 * CAP2
    dk_ref[...] = jnp.concatenate([total[:CAP2], total[third : third + CAP3]], axis=0).astype(BF16)
    dv_ref[...] = jnp.concatenate(
        [total[CAP2 : 2 * CAP2], total[third + CAP3 : third + 2 * CAP3]], axis=0
    ).astype(BF16)
    dw_ref[...] = total[third + PAD3 :]


def on_device(token_picks, live_counts, attn_query, attn_key, attn_value, out_grad, out_weight):
    del token_picks
    vmem = pl.BlockSpec(memory_space=pltpu.VMEM)
    anywhere = pl.BlockSpec(memory_space=pl.ANY)
    parameters = pltpu.CompilerParams(vmem_limit_bytes=32 * 2**20)

    def run(kernel, outs, args):
        return pl.pallas_call(
            kernel,
            out_shape=[jax.ShapeDtypeStruct(*o) for o in outs],
            in_specs=[vmem] * len(args),
            out_specs=[vmem] * len(outs),
            compiler_params=parameters,
        )(*args)

    live_counts = live_counts.T
    kv, out_grad, limits = pl.pallas_call(
        start_kernel,
        out_shape=[
            jax.ShapeDtypeStruct((NF, 2 * SLOTS, WIDTH), BF16),
            jax.ShapeDtypeStruct(out_grad.shape, BF16),
            jax.ShapeDtypeStruct((2 * NF, HS), jnp.int32),
        ],
        in_specs=[anywhere] * 4,
        out_specs=[anywhere, vmem, vmem],
        scratch_shapes=[
            pltpu.SMEM(live_counts.shape, jnp.int32),
            pltpu.VMEM((SLOTS, WIDTH), BF16),
            pltpu.VMEM((SLOTS, WIDTH), BF16),
            pltpu.VMEM(out_grad.shape, BF16),
            pltpu.VMEM((2 * SLOTS, WIDTH), BF16),
            pltpu.SemaphoreType.DMA((4,)),
            pltpu.SemaphoreType.DMA((NF,)),
        ],
    )(live_counts, attn_key, attn_value, out_grad)
    kv = lax.all_to_all(kv, FAR, 0, 0)
    grad = lax.all_gather(out_grad[None], "tp", axis=0, tiled=True, axis_index_groups=[[0, 1], [2, 3]])
    grad = lax.all_gather(grad, "tp", axis=0, tiled=True, axis_index_groups=[[0, 3], [1, 2]])
    (qd,) = run(
        project_kernel, [((ROWS, 2 * WIDTH + MODEL), BF16)], (grad, out_weight, attn_query)
    )
    qd = lax.all_gather(qd, NEAR, axis=0, tiled=False)
    lanes = 2 * NEARS
    stats, *kept = run(
        stats_kernel,
        [((QROWS + 8, WIDTH), F32)]
        + [((NF * slots, lanes * slots), F32) for slots in (CAP2, CAP2, PAD3, PAD3)],
        (limits, kv, qd),
    )
    stats = lax.all_gather(stats, NEAR, axis=0, tiled=False)
    back, dq = run(
        grads_kernel,
        [((NF, BACK, WIDTH), BF16), ((QROWS, WIDTH), F32)],
        (kv, qd, stats, *kept),
    )
    back = lax.all_to_all(back, FAR, 0, 0)
    dq = lax.all_gather(dq, NEAR, axis=0, tiled=False)
    (query_grad,) = run(query_kernel, [((SLOTS, WIDTH), BF16)], (dq,))
    key_grad, value_grad, weight_grad = run(
        last_kernel,
        [((SLOTS, WIDTH), BF16), ((SLOTS, WIDTH), BF16), ((COLS, WIDTH), F32)],
        (back,),
    )
    return query_grad, key_grad, value_grad, weight_grad.T


def solution(mesh):
    grid = Mesh(mesh.devices.reshape(NZ, NY, NX, NC, TP), ("z", "y", "x", "c", "tp"))
    seq = ("z", "y", "x", "c")
    rows = P(seq, "tp")
    return jax.shard_map(
        on_device,
        mesh=grid,
        in_specs=(P(), P(), rows, rows, rows, rows, P("tp", None)),
        out_specs=(rows, rows, rows, P("tp", seq)),
        check_vma=False,
    )
```

time: 88.8 us -> 83.5 us (0.940)
  blocking collectives: 37 us -> 34.3 us
  local copies, waits for them, and re-layouts: 2.34 us -> 0.02 us
    all_gather x1 -> x2, blocking collectives: 14.1 us -> 10.8 us  [the longest x1 6.52 us: on_device(): lax.all_gather(grad, 'tp', axis=0, tiled=True, axis_index_groups=[[0, 3],...]
    pallas_call x0 -> x1, Pallas kernels: none -> 2.6 us  [on_device(): pl.pallas_call(start_kernel, out_shape=[jax.ShapeDtypeStruct((NF, 2 * SLO...]
    pallas_call x5, Pallas kernels: 6.93 us -> 4.37 us  [run(): pl.pallas_call(kernel, out_shape=[jax.ShapeDtypeStruct(*o) for o in outs]...]
    unnamed x8, local copies, waits for them, and re-layouts: 1.41 us -> 0.02 us
    broadcast_in_dim x1 -> x0, local copies, waits for them, and re-layouts: 0.93 us -> none  [on_device(): kv = jnp.broadcast_to(kv[None], (NF, ROWS, 2 * WIDTH))]
  transfers between devices with their start and end apart: 2 -> 2, of which waited for: 1 -> 1; matrix products, arithmetic and copies ran while one was open for 0% -> 0% of each run, Pallas kernels for 2% -> 1%
where the time goes in v3:
time: 83.5 us; the launch traced here: 82.4 us
  blocking collectives  34.3 us (41%)
  starting transfers between devices  23.2 us (28%)
  waiting for transfers between devices  17.2 us (21%)
  Pallas kernels  6.97 us (8%)
    all_to_all x1, waiting for transfers between devices, on_device(): back = lax.all_to_all(back, FAR, 0, 0)  17.2 us
    all_to_all x1, starting transfers between devices, on_device(): kv = lax.all_to_all(kv, FAR, 0, 0)  13.7 us
    all_gather x1, blocking collectives, on_device(): qd = lax.all_gather(qd, NEAR, axis=0, tiled=False)  10.2 us
    all_to_all x1, starting transfers between devices, on_device(): back = lax.all_to_all(back, FAR, 0, 0)  9.49 us
    all_gather x1, blocking collectives, on_device(): stats = lax.all_gather(stats, NEAR, axis=0, tiled=False)  6.75 us
    all_gather x1, blocking collectives, on_device(): dq = lax.all_gather(dq, NEAR, axis=0, tiled=False)  6.58 us
    all_gather x1, blocking collectives, on_device(): lax.all_gather(grad, 'tp', axis=0, tiled=True, axis_index_groups=[[0, 3],...  6.52 us
    pallas_call x5, Pallas kernels, run(): pl.pallas_call(kernel, out_shape=[jax.ShapeDtypeStruct(*o) for o in outs]...  4.37 us
  transfers between devices with their start and end apart: 2, of which 1 were waited for; matrix products, arithmetic and copies ran while one was open for 0% of the time, Pallas kernels for 1%

profile of v3, /device:TPU:1, one launch (start us, length us, event | category | flops | bytes accessed | tf_op | source)
XLA Modules:
  0.0 82.4 jit_solution(10799864679458311204)
XLA Ops:
  0.6 0.0 copy-start
  0.6 2.6 %shard_map.93 = (bf16[32,40,256]{2,1,0:T(8,128)(2,1)}, bf16[20,512]{1,0:T(8,128)(2,1)}, s32[64,128]{1,0:T(8,128)}) custom-call(s32[2,128]{1,0:T(2,128)} %bitcast.11, bf16[20,256]{1,0:T(8,128)(2,1)} %key_any.1, bf16[20,256]{1,0:T(8,128)(2,1)} %value_any.1, bf16[20,512]{1,0:T(8,128)(2,1)} %grad_any.1), custom_call_target="tpu_custom_call" | custom-call | tf_op jit(solution)/shard_map/pallas_call | solution.py:252
  3.2 0.0 copy-start.3
  3.3 13.7 %all-to-all-start = ((bf16[32,40,256]{2,1,0:T(8,128)(2,1)}), bf16[32,40,256]{2,1,0:T(8,128)(2,1)S(1)}, u32[]{:S(2)}, u32[]{:S(2)}) async-start(bf16[32,40,256]{2,1,0:T(8,128)(2,1)} %get-tuple-element.17), calls=%async_computation | async-start | bytes 1310720 | tf_op jit(solution)/shard_map/all_to_all | solution.py:271
  17.0 0.0 copy-done.3
  17.0 4.3 %all-gather.4 = bf16[2,20,512]{2,1,0:T(8,128)(2,1)S(1)} all-gather(bf16[1,20,512]{2,1,0:T(8,128)(2,1)S(1)} %bitcast.10), channel_id=2, replica_groups={{0,1},{2,3},{4,5},{6,7},{8,9},{10,11},{12,13},{14,15},{16,17},{18,19},{..., dimensions={0}, use_global_device_ids=true | all-gather | bytes 61440 | tf_op jit(solution)/shard_map/all_gather | solution.py:272
  21.3 0.0 copy-start.2
  21.3 6.5 %all_gather.25.grad_ref = bf16[4,20,512]{2,1,0:T(8,128)(2,1)S(1)} all-gather(bf16[2,20,512]{2,1,0:T(8,128)(2,1)S(1)} %all-gather.4), channel_id=1, replica_groups={{0,3},{1,2},{4,7},{5,6},{8,11},{9,10},{12,15},{13,14},{16,19},{17,18},{..., dimensions={0}, use_global_device_ids=true | all-gather | bytes 122880 | tf_op jit(solution)/shard_map/all_gather | solution.py:273
  27.8 0.0 copy-done
  27.8 0.0 copy-done.2
  27.8 0.4 shard_map.94
  28.2 0.0 copy-start.1
  28.2 10.2 %all-gather.1 = bf16[96,2560]{1,0:T(8,128)(2,1)S(1)} all-gather(bf16[24,2560]{1,0:T(8,128)(2,1)S(1)} %shard_map.94), channel_id=3, replica_groups=mesh['z'=8,'y'=2,'x'=4,'c'=2,'tp'=4] {'y','c'}, dimensions={0}, use_global_device_ids=true | all-gather | bytes 614400 | tf_op jit(solution)/shard_map/all_gather | solution.py:277
  38.3 0.0 all-to-all-done.kv_ref
  38.3 0.0 copy-done.1
  38.3 1.0 %shard_map.95 = (f32[104,256]{1,0:T(8,128)S(1)}, f32[512,128]{1,0:T(8,128)S(1)}, f32[512,128]{1,0:T(8,128)S(1)}, f32[256,64]{1,0:T(8,128)S(1)}, f32[256,64]{1,0:T(8,128)S(1)}) custom-call(s32[64,128]{1,0:T(8,128)S(1)} %copy-done.1, bf16[32,40,256]{2,1,0:T(8,128)(2,1)S(1)} %all-to-all-done.kv_ref, bf16[4,24,2560]{2,1,0:T(8,128)(2,1)S(1)} %bitcast.6), custom_call_target="tpu_custom_call" | custom-call | tf_op jit(solution)/shard_map/pallas_call | solution.py:243
  39.3 6.8 %all-gather.2 = f32[416,256]{1,0:T(8,128)S(1)} all-gather(f32[104,256]{1,0:T(8,128)S(1)} %get-tuple-element.20), channel_id=4, replica_groups=mesh['z'=8,'y'=2,'x'=4,'c'=2,'tp'=4] {'y','c'}, dimensions={0}, use_global_device_ids=true | all-gather | bytes 532480 | tf_op jit(solution)/shard_map/all_gather | solution.py:285
  46.1 1.6 %shard_map.96 = (bf16[32,56,256]{2,1,0:T(8,128)(2,1)}, f32[96,256]{1,0:T(8,128)S(1)}) custom-call(bf16[32,40,256]{2,1,0:T(8,128)(2,1)S(1)} %all-to-all-done.kv_ref, bf16[4,24,2560]{2,1,0:T(8,128)(2,1)S(1)} %bitcast.7, f32[4,104,256]{2,1,0:T(8,128)S(1)} %bitcast.8, f32[512,128]{1,0:T(8,128)S(1)} %get-tuple-element.21.refs_0_, ...), custom_call_target="tpu_custom_call" | custom-call | tf_op jit(solution)/shard_map/pallas_call | solution.py:243
  47.7 9.5 %all-to-all-start.1 = ((bf16[32,56,256]{2,1,0:T(8,128)(2,1)}), bf16[32,56,256]{2,1,0:T(8,128)(2,1)S(1)}, u32[]{:S(2)}, u32[]{:S(2)}) async-start(bf16[32,56,256]{2,1,0:T(8,128)(2,1)} %get-tuple-element.26), calls=%async_computation.1 | async-start | bytes 1835008 | tf_op jit(solution)/shard_map/all_to_all | solution.py:291
  57.2 6.6 %all-gather.3 = f32[384,256]{1,0:T(8,128)S(1)} all-gather(f32[96,256]{1,0:T(8,128)S(1)} %get-tuple-element.25), channel_id=5, replica_groups=mesh['z'=8,'y'=2,'x'=4,'c'=2,'tp'=4] {'y','c'}, dimensions={0}, use_global_device_ids=true | all-gather | bytes 491520 | tf_op jit(solution)/shard_map/all_gather | solution.py:292
  63.8 0.6 shard_map.97
  64.4 17.2 %all-to-all-done.1.in_ref = bf16[32,56,256]{2,1,0:T(8,128)(2,1)S(1)} async-done(((bf16[32,56,256]{2,1,0:T(8,128)(2,1)}), bf16[32,56,256]{2,1,0:T(8,128)(2,1)S(1)}, u32[]{:S(2)}, u32[]{:S(2)}) %all-to-all-start.1) | async-done | bytes 917536 | tf_op jit(solution)/shard_map/all_to_all | solution.py:291
  81.6 0.7 shard_map.98
Async XLA Ops:
  0.6 27.2 %copy-start = (bf16[256,2048]{1,0:T(8,128)(2,1)S(1)}, bf16[256,2048]{1,0:T(8,128)(2,1)}, u32[]{:S(2)}) copy-start(bf16[256,2048]{1,0:T(8,128)(2,1)} %weight_ref.1) | copy-start | bytes 3145732
  3.2 13.7 %copy-start.3 = (bf16[20,512]{1,0:T(8,128)(2,1)S(1)}, bf16[20,512]{1,0:T(8,128)(2,1)}, u32[]{:S(2)}) copy-start(bf16[20,512]{1,0:T(8,128)(2,1)} %get-tuple-element.18) | copy-start | bytes 61444
  3.3 35.1 %all-to-all-start = ((bf16[32,40,256]{2,1,0:T(8,128)(2,1)}), bf16[32,40,256]{2,1,0:T(8,128)(2,1)S(1)}, u32[]{:S(2)}, u32[]{:S(2)}) async-start(bf16[32,40,256]{2,1,0:T(8,128)(2,1)} %get-tuple-element.17), calls=%async_computation | async-start | bytes 1310720 | tf_op jit(solution)/shard_map/all_to_all | solution.py:271
  21.3 6.5 %copy-start.2 = (bf16[20,256]{1,0:T(8,128)(2,1)S(1)}, bf16[20,256]{1,0:T(8,128)(2,1)}, u32[]{:S(2)}) copy-start(bf16[20,256]{1,0:T(8,128)(2,1)} %query_ref.1) | copy-start | bytes 30724
  28.2 10.2 %copy-start.1 = (s32[64,128]{1,0:T(8,128)S(1)}, s32[64,128]{1,0:T(8,128)}, u32[]{:S(2)}) copy-start(s32[64,128]{1,0:T(8,128)} %get-tuple-element.19.limit_ref) | copy-start | bytes 98308
  47.7 33.9 %all-to-all-start.1 = ((bf16[32,56,256]{2,1,0:T(8,128)(2,1)}), bf16[32,56,256]{2,1,0:T(8,128)(2,1)S(1)}, u32[]{:S(2)}, u32[]{:S(2)}) async-start(bf16[32,56,256]{2,1,0:T(8,128)(2,1)} %get-tuple-element.26), calls=%async_computation.1 | async-start | bytes 1835008 | tf_op jit(solution)/shard_map/all_to_all | solution.py:291

commit v4 on v3

--- a/solution.py
+++ b/solution.py
@@ -22,6 +22,9 @@
 COLS = MODEL // 128
 QROWS = NEARS * ROWS
 BACK = 2 * CAP2 + PAD3 + COLS
+PIECES = 3
+STATS = 16
+BATCH = 8
 SCALE = HS**-0.5
 LOW = -1e30
 F32 = jnp.float32
@@ -114,10 +117,15 @@
     moves[0].wait()
     moves[1].wait()
     keys, values = key[...].astype(F32), value[...].astype(F32)
-    block[...] = jnp.concatenate(
+    packed = jnp.concatenate(
         [keys[:CAP2], values[:CAP2], keys[CAP2:], values[CAP2:]], axis=0
     ).astype(BF16)
-    sends = [pltpu.make_async_copy(block, kv_any.at[f], out_sems.at[f]) for f in range(NF)]
+    for i in range(BATCH):
+        block[i] = packed
+    sends = [
+        pltpu.make_async_copy(block, kv_any.at[i * BATCH : (i + 1) * BATCH], out_sems.at[i])
+        for i in range(NF // BATCH)
+    ]
     for send in sends:
         send.start()
     moves[2].wait()
@@ -162,23 +170,31 @@
         logs = jnp.where(none, LOW, top + jnp.log(jnp.where(none, 1.0, total)))
         delta = jnp.sum(weights * dprob, axis=0, keepdims=True)
         attended = head_blocks(mm(weights.astype(BF16), value, TN))
-        out_ref[start : start + NEARS * slots] = attended
+        out_ref[start : start + NEARS * slots] = attended.astype(BF16)
         start += NEARS * slots
-        rest = jnp.zeros((1, WIDTH - logs.shape[1]), F32)
-        stats += [jnp.concatenate([logs, rest], axis=1), jnp.concatenate([delta, rest], axis=1)]
-    out_ref[start:] = jnp.concatenate(stats + [jnp.zeros((8 - len(stats), WIDTH), F32)], axis=0)
+        for row in (logs, delta):
+            row = jnp.concatenate([row, jnp.zeros((1, WIDTH - row.shape[1]), F32)], axis=1)
+            for _ in range(PIECES):
+                piece = row.astype(BF16).astype(F32)
+                stats.append(piece)
+                row = row - piece
+    rest = jnp.zeros((STATS - len(stats), WIDTH), F32)
+    out_ref[start:] = jnp.concatenate(stats + [rest], axis=0).astype(BF16)
 
 
 def grads_kernel(kv_ref, qd_ref, in_ref, *refs):
     kept, (out_ref, dq_ref) = refs[:4], refs[4:]
     _, y, _, c = place()
+    lines = in_ref[:, QROWS:].astype(F32)
     attended = []
     d_key, d_value = [], []
     start = 0
     for which, slots, key, _, query, d_attn in blocks(kv_ref, qd_ref):
         count = NEARS * slots
-        logs = in_ref[:, QROWS + 2 * which, : 2 * count]
-        deltas = in_ref[:, QROWS + 2 * which + 1, : 2 * count]
+        logs, deltas = (
+            jnp.sum(lines[:, first : first + PIECES, : 2 * count], axis=1)
+            for first in (2 * which * PIECES, (2 * which + 1) * PIECES)
+        )
         top = jnp.max(logs, axis=0, keepdims=True)
         log_total = top + jnp.log(jnp.sum(jnp.exp(logs - top), axis=0, keepdims=True))
         share = jnp.exp(logs - log_total)
@@ -188,7 +204,7 @@
         total = jnp.zeros((count, WIDTH), F32)
         for n in range(NEARS):
             own = jnp.where(column < HS, share_down[:count, n : n + 1], share_down[count:, n : n + 1])
-            total += own * in_ref[n, start : start + count]
+            total += own * in_ref[n, start : start + count].astype(F32)
         attended.append(total)
 
         prob = jnp.exp(kept[2 * which][...] - log_total)
@@ -263,9 +279,9 @@
             pltpu.VMEM((SLOTS, WIDTH), BF16),
             pltpu.VMEM((SLOTS, WIDTH), BF16),
             pltpu.VMEM(out_grad.shape, BF16),
-            pltpu.VMEM((2 * SLOTS, WIDTH), BF16),
+            pltpu.VMEM((BATCH, 2 * SLOTS, WIDTH), BF16),
             pltpu.SemaphoreType.DMA((4,)),
-            pltpu.SemaphoreType.DMA((NF,)),
+            pltpu.SemaphoreType.DMA((NF // BATCH,)),
         ],
     )(live_counts, attn_key, attn_value, out_grad)
     kv = lax.all_to_all(kv, FAR, 0, 0)
@@ -278,7 +294,7 @@
     lanes = 2 * NEARS
     stats, *kept = run(
         stats_kernel,
-        [((QROWS + 8, WIDTH), F32)]
+        [((QROWS + STATS, WIDTH), BF16)]
         + [((NF * slots, lanes * slots), F32) for slots in (CAP2, CAP2, PAD3, PAD3)],
         (limits, kv, qd),
     )

time: 83.5 us -> 82.2 us (0.984)
  blocking collectives: 34.3 us -> 33.2 us
    all_gather x1, blocking collectives: 6.75 us -> 5.69 us  [on_device(): stats = lax.all_gather(stats, NEAR, axis=0, tiled=False)]
where the time goes in v4:
time: 82.2 us; the launch traced here: 81 us
  blocking collectives  33.2 us (40%)
  starting transfers between devices  23.2 us (28%)
  waiting for transfers between devices  17.2 us (21%)
  Pallas kernels  6.72 us (8%)
    all_to_all x1, waiting for transfers between devices, on_device(): back = lax.all_to_all(back, FAR, 0, 0)  17.2 us
    all_to_all x1, starting transfers between devices, on_device(): kv = lax.all_to_all(kv, FAR, 0, 0)  13.7 us
    all_gather x1, blocking collectives, on_device(): qd = lax.all_gather(qd, NEAR, axis=0, tiled=False)  10.2 us
    all_to_all x1, starting transfers between devices, on_device(): back = lax.all_to_all(back, FAR, 0, 0)  9.49 us
    all_gather x1, blocking collectives, on_device(): dq = lax.all_gather(dq, NEAR, axis=0, tiled=False)  6.58 us
    all_gather x1, blocking collectives, on_device(): lax.all_gather(grad, 'tp', axis=0, tiled=True, axis_index_groups=[[0, 3],...  6.52 us
    all_gather x1, blocking collectives, on_device(): stats = lax.all_gather(stats, NEAR, axis=0, tiled=False)  5.69 us
    pallas_call x5, Pallas kernels, run(): pl.pallas_call(kernel, out_shape=[jax.ShapeDtypeStruct(*o) for o in outs]...  4.36 us
  transfers between devices with their start and end apart: 2, of which 1 were waited for; matrix products, arithmetic and copies ran while one was open for 0% of the time, Pallas kernels for 1%

profile of v4, /device:TPU:1, one launch (start us, length us, event | category | flops | bytes accessed | tf_op | source)
XLA Modules:
  0.0 81.0 jit_solution(12740180986261541971)
XLA Ops:
  0.6 0.0 copy-start
  0.6 2.4 %shard_map.93 = (bf16[32,40,256]{2,1,0:T(8,128)(2,1)}, bf16[20,512]{1,0:T(8,128)(2,1)}, s32[64,128]{1,0:T(8,128)}) custom-call(s32[2,128]{1,0:T(2,128)} %bitcast.11, bf16[20,256]{1,0:T(8,128)(2,1)} %key_any.1, bf16[20,256]{1,0:T(8,128)(2,1)} %value_any.1, bf16[20,512]{1,0:T(8,128)(2,1)} %grad_any.1), custom_call_target="tpu_custom_call" | custom-call | tf_op jit(solution)/shard_map/pallas_call | solution.py:268
  3.0 0.0 copy-start.3
  3.0 13.7 %all-to-all-start = ((bf16[32,40,256]{2,1,0:T(8,128)(2,1)}), bf16[32,40,256]{2,1,0:T(8,128)(2,1)S(1)}, u32[]{:S(2)}, u32[]{:S(2)}) async-start(bf16[32,40,256]{2,1,0:T(8,128)(2,1)} %get-tuple-element.17), calls=%async_computation | async-start | bytes 1310720 | tf_op jit(solution)/shard_map/all_to_all | solution.py:287
  16.7 0.0 copy-done.3
  16.8 4.3 %all-gather.4 = bf16[2,20,512]{2,1,0:T(8,128)(2,1)S(1)} all-gather(bf16[1,20,512]{2,1,0:T(8,128)(2,1)S(1)} %bitcast.10), channel_id=2, replica_groups={{0,1},{2,3},{4,5},{6,7},{8,9},{10,11},{12,13},{14,15},{16,17},{18,19},{..., dimensions={0}, use_global_device_ids=true | all-gather | bytes 61440 | tf_op jit(solution)/shard_map/all_gather | solution.py:288
  21.0 0.0 copy-start.2
  21.0 6.5 %all_gather.25.grad_ref = bf16[4,20,512]{2,1,0:T(8,128)(2,1)S(1)} all-gather(bf16[2,20,512]{2,1,0:T(8,128)(2,1)S(1)} %all-gather.4), channel_id=1, replica_groups={{0,3},{1,2},{4,7},{5,6},{8,11},{9,10},{12,15},{13,14},{16,19},{17,18},{..., dimensions={0}, use_global_device_ids=true | all-gather | bytes 122880 | tf_op jit(solution)/shard_map/all_gather | solution.py:289
  27.5 0.0 copy-done
  27.5 0.0 copy-done.2
  27.5 0.4 shard_map.94
  27.9 0.0 copy-start.1
  27.9 10.2 %all-gather.1 = bf16[96,2560]{1,0:T(8,128)(2,1)S(1)} all-gather(bf16[24,2560]{1,0:T(8,128)(2,1)S(1)} %shard_map.94), channel_id=3, replica_groups=mesh['z'=8,'y'=2,'x'=4,'c'=2,'tp'=4] {'y','c'}, dimensions={0}, use_global_device_ids=true | all-gather | bytes 614400 | tf_op jit(solution)/shard_map/all_gather | solution.py:293
  38.1 0.0 all-to-all-done.kv_ref
  38.1 0.0 copy-done.1
  38.1 1.0 %shard_map.95 = (bf16[112,256]{1,0:T(8,128)(2,1)S(1)}, f32[512,128]{1,0:T(8,128)S(1)}, f32[512,128]{1,0:T(8,128)S(1)}, f32[256,64]{1,0:T(8,128)S(1)}, f32[256,64]{1,0:T(8,128)S(1)}) custom-call(s32[64,128]{1,0:T(8,128)S(1)} %copy-done.1, bf16[32,40,256]{2,1,0:T(8,128)(2,1)S(1)} %all-to-all-done.kv_ref, bf16[4,24,2560]{2,1,0:T(8,128)(2,1)S(1)} %bitcast.6), custom_call_target="tpu_custom_call" | custom-call | tf_op jit(solution)/shard_map/pallas_call | solution.py:259
  39.1 5.7 %all-gather.2 = bf16[448,256]{1,0:T(8,128)(2,1)S(1)} all-gather(bf16[112,256]{1,0:T(8,128)(2,1)S(1)} %get-tuple-element.20), channel_id=4, replica_groups=mesh['z'=8,'y'=2,'x'=4,'c'=2,'tp'=4] {'y','c'}, dimensions={0}, use_global_device_ids=true | all-gather | bytes 286720 | tf_op jit(solution)/shard_map/all_gather | solution.py:301
  44.8 1.7 %shard_map.96 = (bf16[32,56,256]{2,1,0:T(8,128)(2,1)}, f32[96,256]{1,0:T(8,128)S(1)}) custom-call(bf16[32,40,256]{2,1,0:T(8,128)(2,1)S(1)} %all-to-all-done.kv_ref, bf16[4,24,2560]{2,1,0:T(8,128)(2,1)S(1)} %bitcast.7, bf16[4,112,256]{2,1,0:T(8,128)(2,1)S(1)} %bitcast.9, f32[512,128]{1,0:T(8,128)S(1)} %get-tuple-element.21.refs_0_, ...), custom_call_target="tpu_custom_call" | custom-call | tf_op jit(solution)/shard_map/pallas_call | solution.py:259
  46.4 9.5 %all-to-all-start.1 = ((bf16[32,56,256]{2,1,0:T(8,128)(2,1)}), bf16[32,56,256]{2,1,0:T(8,128)(2,1)S(1)}, u32[]{:S(2)}, u32[]{:S(2)}) async-start(bf16[32,56,256]{2,1,0:T(8,128)(2,1)} %get-tuple-element.26), calls=%async_computation.1 | async-start | bytes 1835008 | tf_op jit(solution)/shard_map/all_to_all | solution.py:307
  55.9 6.6 %all-gather.3 = f32[384,256]{1,0:T(8,128)S(1)} all-gather(f32[96,256]{1,0:T(8,128)S(1)} %get-tuple-element.25), channel_id=5, replica_groups=mesh['z'=8,'y'=2,'x'=4,'c'=2,'tp'=4] {'y','c'}, dimensions={0}, use_global_device_ids=true | all-gather | bytes 491520 | tf_op jit(solution)/shard_map/all_gather | solution.py:308
  62.5 0.6 shard_map.97
  63.1 17.2 %all-to-all-done.1.in_ref = bf16[32,56,256]{2,1,0:T(8,128)(2,1)S(1)} async-done(((bf16[32,56,256]{2,1,0:T(8,128)(2,1)}), bf16[32,56,256]{2,1,0:T(8,128)(2,1)S(1)}, u32[]{:S(2)}, u32[]{:S(2)}) %all-to-all-start.1) | async-done | bytes 917536 | tf_op jit(solution)/shard_map/all_to_all | solution.py:307
  80.3 0.7 shard_map.98
Async XLA Ops:
  0.6 26.9 %copy-start = (bf16[256,2048]{1,0:T(8,128)(2,1)S(1)}, bf16[256,2048]{1,0:T(8,128)(2,1)}, u32[]{:S(2)}) copy-start(bf16[256,2048]{1,0:T(8,128)(2,1)} %weight_ref.1) | copy-start | bytes 3145732
  3.0 13.7 %copy-start.3 = (bf16[20,512]{1,0:T(8,128)(2,1)S(1)}, bf16[20,512]{1,0:T(8,128)(2,1)}, u32[]{:S(2)}) copy-start(bf16[20,512]{1,0:T(8,128)(2,1)} %get-tuple-element.18) | copy-start | bytes 61444
  3.0 35.1 %all-to-all-start = ((bf16[32,40,256]{2,1,0:T(8,128)(2,1)}), bf16[32,40,256]{2,1,0:T(8,128)(2,1)S(1)}, u32[]{:S(2)}, u32[]{:S(2)}) async-start(bf16[32,40,256]{2,1,0:T(8,128)(2,1)} %get-tuple-element.17), calls=%async_computation | async-start | bytes 1310720 | tf_op jit(solution)/shard_map/all_to_all | solution.py:287
  21.0 6.5 %copy-start.2 = (bf16[20,256]{1,0:T(8,128)(2,1)S(1)}, bf16[20,256]{1,0:T(8,128)(2,1)}, u32[]{:S(2)}) copy-start(bf16[20,256]{1,0:T(8,128)(2,1)} %query_ref.1) | copy-start | bytes 30724
  27.9 10.2 %copy-start.1 = (s32[64,128]{1,0:T(8,128)S(1)}, s32[64,128]{1,0:T(8,128)}, u32[]{:S(2)}) copy-start(s32[64,128]{1,0:T(8,128)} %get-tuple-element.19.limit_ref) | copy-start | bytes 98308
  46.4 33.9 %all-to-all-start.1 = ((bf16[32,56,256]{2,1,0:T(8,128)(2,1)}), bf16[32,56,256]{2,1,0:T(8,128)(2,1)S(1)}, u32[]{:S(2)}, u32[]{:S(2)}) async-start(bf16[32,56,256]{2,1,0:T(8,128)(2,1)} %get-tuple-element.26), calls=%async_computation.1 | async-start | bytes 1835008 | tf_op jit(solution)/shard_map/all_to_all | solution.py:307

commit v5 on v4

v5 whole, which is shorter than its diff:
```python
import jax
import jax.numpy as jnp
from jax import lax
from jax.experimental import pallas as pl
from jax.experimental.pallas import tpu as pltpu
from jax.sharding import Mesh
from jax.sharding import PartitionSpec as P

HS = 128
NZ, NY, NX, NC = 8, 2, 4, 2
FAR = ("z", "x")
NEAR = ("y", "c")
NF, NEARS = NZ * NX, NY * NC
TP = 4
SLOTS = 20
CAP2 = 16
CAP3 = 4
PAD3 = 8
ROWS = CAP2 + PAD3
WIDTH = 2 * HS
MODEL = 2048
COLS = MODEL // 128
QROWS = NEARS * ROWS
BACK = 2 * CAP2 + PAD3 + COLS
PIECES = 3
STATS = 16
PART = 8
BATCH = 8
SCALE = HS**-0.5
LOW = -1e30
F32 = jnp.float32
BF16 = jnp.bfloat16

NT = (((1,), (1,)), ((), ()))
NN = (((1,), (0,)), ((), ()))
TN = (((0,), (0,)), ((), ()))


def mm(left, right, dims):
    return lax.dot_general(left, right, dims, preferred_element_type=F32)


def split_rows(block):
    wide = block.astype(F32)
    count, _, width = wide.shape
    second = wide[:, :CAP2].reshape(count * CAP2, width).astype(BF16)
    third = wide[:, CAP2:].reshape(count * PAD3, width).astype(BF16)
    return second, third


def by_head(rows):
    column = lax.broadcasted_iota(jnp.int32, rows.shape, 1)
    zero = jnp.zeros_like(rows)
    return jnp.concatenate(
        [jnp.where(column < HS, rows, zero), jnp.where(column < HS, zero, rows)], axis=0
    )


def head_blocks(both):
    count = both.shape[0] // 2
    column = lax.broadcasted_iota(jnp.int32, (count, WIDTH), 1)
    return jnp.where(column < HS, both[:count], both[count:])


def shard_of(z, y, x, c):
    return ((z * NY + y) * NX + x) * NC + c


def place():
    return tuple(lax.axis_index(axis) for axis in ("z", "y", "x", "c"))


def allowed(limit_ref, which, slots):
    z, y, x, c = place()
    shape = (NF * slots, 2 * NEARS * slots)
    key_row = lax.broadcasted_iota(jnp.int32, shape, 0)
    query_row = lax.broadcasted_iota(jnp.int32, shape, 1) % (NEARS * slots)
    key_far, key_slot = key_row // slots, key_row % slots
    key_shard = shard_of(key_far // NX, y, key_far % NX, c)
    near, query_slot = query_row // slots, query_row % slots
    query_shard = shard_of(z, near // NC, x, near % NC)
    limit = limit_ref[which * NF : (which + 1) * NF, : shape[1]]
    limit = jnp.broadcast_to(limit[:, None, :], (NF, slots, shape[1])).reshape(shape)
    in_order = key_shard * slots + key_slot <= query_shard * slots + query_slot
    return in_order & (key_slot < limit)


def padded(block):
    rest = jnp.zeros((ROWS - SLOTS, block.shape[1]), F32)
    return jnp.concatenate([block.astype(F32), rest], axis=0).astype(BF16)


def start_kernel(
    counts_any, key_any, value_any, kv_any, live_any, limit_any, counts, key, value, block, live, limits, sems, out_sems
):
    moves = [
        pltpu.make_async_copy(source, target, sems.at[i])
        for i, (source, target) in enumerate(((key_any, key), (value_any, value), (counts_any, counts)))
    ]
    for move in moves:
        move.start()
    moves[0].wait()
    moves[1].wait()
    keys, values = key[...].astype(F32), value[...].astype(F32)
    packed = jnp.concatenate(
        [keys[:CAP2], values[:CAP2], keys[CAP2:], values[CAP2:]], axis=0
    ).astype(BF16)
    for i in range(BATCH):
        block[i] = packed
    batches = NF // BATCH
    sends = [
        pltpu.make_async_copy(block, kv_any.at[i * BATCH : (i + 1) * BATCH], out_sems.at[i])
        for i in range(batches)
    ]
    for send in sends:
        send.start()
    moves[2].wait()
    z, y, x, c = place()
    shard = shard_of(z, y, x, c)
    slot = lax.broadcasted_iota(jnp.int32, live.shape, 0)
    limit = jnp.where(slot < CAP2, counts[0, shard], CAP2 + counts[1, shard])
    live[...] = jnp.where(slot < limit, 1.0, 0.0)
    for which in range(2):
        for f in range(NF):
            limit = counts[which, shard_of(f // NX, y, f % NX, c)]
            limits[which * NF + f : which * NF + f + 1, :] = jnp.full((1, HS), limit, jnp.int32)
    rest = [
        pltpu.make_async_copy(live, live_any, out_sems.at[batches]),
        pltpu.make_async_copy(limits, limit_any, out_sems.at[batches + 1]),
    ]
    for send in rest:
        send.start()
    for send in sends + rest:
        send.wait()


def pair_kernel(own_ref, other_ref, out_ref):
    out_ref[0] = own_ref[...]
    out_ref[1] = other_ref[...]


def project_kernel(live_ref, grad_ref, weight_ref, query_ref, out_ref):
    me = lax.axis_index("tp")
    outer = (me == 0) | (me == 3)
    first, second = jnp.where(outer, 0, 1), jnp.where(outer, 3, 2)
    live = live_ref[:, :1]
    total = jnp.zeros((ROWS, WIDTH), F32)
    for k, t in enumerate((first, 1 - first, second, 5 - second)):
        column = pl.multiple_of(t * 512, 512)
        wide = jnp.concatenate(
            [grad_ref[k].astype(F32), jnp.zeros((ROWS - SLOTS, 512), F32)], axis=0
        )
        piece = (wide * live).astype(BF16)
        total += mm(piece, weight_ref[:, pl.ds(column, 512)], NT)
        out_ref[:, pl.ds(2 * WIDTH + column, 512)] = piece
    out_ref[:, :WIDTH] = padded(query_ref[...])
    out_ref[:, WIDTH : 2 * WIDTH] = total.astype(BF16)


def prepare_kernel(limit_ref, qd_ref, *refs):
    _, y, _, c = place()
    qd_parts = split_rows(qd_ref[:, :, : 2 * WIDTH])
    for which, slots in ((0, CAP2), (1, PAD3)):
        query_ref, d_attn_ref, bias_ref = refs[3 * which : 3 * which + 3]
        query_ref[...] = by_head(qd_parts[which][:, :WIDTH])
        d_attn_ref[...] = by_head(qd_parts[which][:, WIDTH:])
        bias_ref[...] = jnp.where(allowed(limit_ref, which, slots), 0.0, LOW)
    columns_ref = refs[6]
    for z in range(NZ):
        column = pl.multiple_of(2 * WIDTH + (z * NY + y) * HS, HS)
        wide = qd_ref[:, :, pl.ds(column, HS)].astype(F32)
        rows = jnp.concatenate(
            [wide[:, :CAP2].reshape(NEARS * CAP2, HS), wide[:, CAP2:].reshape(NEARS * PAD3, HS)], axis=0
        )
        down = rows.T.reshape(NX, NC, COLS, QROWS)
        own = jnp.where(c == 0, down[:, 0], down[:, 1]).reshape(NX * COLS, QROWS)
        columns_ref[z * NX * COLS : (z + 1) * NX * COLS] = own.astype(BF16)


def unpacked(kv_ref):
    third = kv_ref[:, 2 * CAP2 :].astype(F32)
    shifted = jnp.concatenate([third[:, CAP3:], third[:, :CAP3]], axis=1)
    second = (kv_ref[:, :CAP2].reshape(NF * CAP2, WIDTH), kv_ref[:, CAP2 : 2 * CAP2].reshape(NF * CAP2, WIDTH))
    return (second, tuple(part.reshape(NF * PAD3, WIDTH).astype(BF16) for part in (third, shifted)))


def stats_kernel(kv_ref, *refs):
    ready, out_ref, kept = refs[:6], refs[6], refs[7:]
    kv = unpacked(kv_ref)
    start = 0
    stats = []
    for which, slots in ((0, CAP2), (1, PAD3)):
        key, value = kv[which]
        query, d_attn, bias = (ref[...] for ref in ready[3 * which : 3 * which + 3])
        scores = mm(key, query, NT) * SCALE + bias
        dprob = mm(value, d_attn, NT)
        kept[2 * which][...] = scores
        kept[2 * which + 1][...] = dprob
        top = jnp.max(scores, axis=0, keepdims=True)
        weights = jnp.exp(scores - top)
        total = jnp.sum(weights, axis=0, keepdims=True)
        weights = weights * (1.0 / total)
        logs = jnp.where(top < 0.5 * LOW, LOW, top + jnp.log(total))
        delta = jnp.sum(weights * dprob, axis=0, keepdims=True)
        attended = head_blocks(mm(weights.astype(BF16), value, TN))
        out_ref[start : start + NEARS * slots] = attended.astype(BF16)
        start += NEARS * slots
        for row in (logs, delta):
            row = jnp.concatenate([row, jnp.zeros((1, WIDTH - row.shape[1]), F32)], axis=1)
            for _ in range(PIECES):
                piece = row.astype(BF16).astype(F32)
                stats.append(piece)
                row = row - piece
    rest = jnp.zeros((STATS - len(stats), WIDTH), F32)
    out_ref[start:] = jnp.concatenate(stats + [rest], axis=0).astype(BF16)


def grads_kernel(in_ref, *refs):
    ready, columns_ref, kept, out_any, dscore_refs = refs[:4], refs[4], refs[5:9], refs[9], refs[10:12]
    block, sems = refs[12:]
    lines = in_ref[:, QROWS:].astype(F32)
    attended, totals = [], []
    start = 0
    for which, slots in ((0, CAP2), (1, PAD3)):
        count = NEARS * slots
        logs, deltas = (
            jnp.sum(lines[:, first : first + PIECES, : 2 * count], axis=1)
            for first in (2 * which * PIECES, (2 * which + 1) * PIECES)
        )
        top = jnp.max(logs, axis=0, keepdims=True)
        log_total = top + jnp.log(jnp.sum(jnp.exp(logs - top), axis=0, keepdims=True))
        share = jnp.exp(logs - log_total)
        totals.append((log_total, jnp.sum(share * deltas, axis=0, keepdims=True)))
        share_down = jnp.concatenate([share, jnp.zeros((8 - NEARS, 2 * count), F32)], axis=0).T
        column = lax.broadcasted_iota(jnp.int32, (count, WIDTH), 1)
        total = jnp.zeros((count, WIDTH), F32)
        for n in range(NEARS):
            own = jnp.where(column < HS, share_down[:count, n : n + 1], share_down[count:, n : n + 1])
            total += own * in_ref[n, start : start + count].astype(F32)
        attended.append(total)
        start += count
    attended = jnp.concatenate(attended, axis=0).astype(BF16)

    sends = []
    for i in range(NF // PART):
        parts = slice(i * PART, (i + 1) * PART)
        third = []
        for which, slots in ((0, CAP2), (1, PAD3)):
            query, d_attn = (ref[...] for ref in ready[2 * which : 2 * which + 2])
            log_total, delta = totals[which]
            keys = slice(i * PART * slots, (i + 1) * PART * slots)
            prob = jnp.exp(kept[2 * which][keys] - log_total)
            dscore = (prob * (kept[2 * which + 1][keys] - delta)).astype(BF16)
            dscore_refs[which][keys] = dscore
            d_key = (mm(dscore, query, NN) * SCALE).reshape(PART, slots, WIDTH)
            d_value = mm(prob.astype(BF16), d_attn, NN).reshape(PART, slots, WIDTH)
            if which == 0:
                block[parts, :CAP2] = d_key.astype(BF16)
                block[parts, CAP2 : 2 * CAP2] = d_value.astype(BF16)
            else:
                third = [d_key[:, :CAP3], d_value[:, :CAP3]]
        columns = columns_ref[i * PART * COLS : (i + 1) * PART * COLS]
        own = mm(columns, attended, NN).reshape(PART, COLS, WIDTH)
        block[parts, 2 * CAP2 :] = jnp.concatenate([*third, own], axis=1).astype(BF16)
        sends.append(pltpu.make_async_copy(block.at[parts], out_any.at[parts], sems.at[i]))
        sends[-1].start()
    for send in sends:
        send.wait()


def partial_kernel(kv_ref, dscore2_ref, dscore3_ref, out_ref):
    start = 0
    for (key, _), dscore_ref in zip(unpacked(kv_ref), (dscore2_ref, dscore3_ref)):
        count = dscore_ref.shape[1] // 2
        out_ref[start : start + count] = head_blocks(mm(dscore_ref[...], key, TN)) * SCALE
        start += count


def query_kernel(in_ref, dq_ref):
    _, y, _, c = place()
    near = y * NC + c
    second = pl.ds(pl.multiple_of(near * CAP2, CAP2), CAP2)
    third = pl.ds(pl.multiple_of(NEARS * CAP2 + near * PAD3, PAD3), PAD3)
    total = jnp.concatenate(
        [jnp.sum(in_ref[:, second, :], axis=0), jnp.sum(in_ref[:, third, :], axis=0)[:CAP3]], axis=0
    )
    dq_ref[...] = total.astype(BF16)


def last_kernel(in_ref, dk_ref, dv_ref, dw_ref):
    total = jnp.sum(in_ref[...].astype(F32), axis=0)
    third = 2 * CAP2
    dk_ref[...] = jnp.concatenate([total[:CAP2], total[third : third + CAP3]], axis=0).astype(BF16)
    dv_ref[...] = jnp.concatenate(
        [total[CAP2 : 2 * CAP2], total[third + CAP3 : third + 2 * CAP3]], axis=0
    ).astype(BF16)
    dw_ref[...] = total[third + PAD3 :]


def on_device(token_picks, live_counts, attn_query, attn_key, attn_value, out_grad, out_weight):
    del token_picks
    vmem = pl.BlockSpec(memory_space=pltpu.VMEM)
    anywhere = pl.BlockSpec(memory_space=pl.ANY)
    parameters = pltpu.CompilerParams(vmem_limit_bytes=32 * 2**20)

    def run(kernel, outs, args):
        return pl.pallas_call(
            kernel,
            out_shape=[jax.ShapeDtypeStruct(*o) for o in outs],
            in_specs=[vmem] * len(args),
            out_specs=[vmem] * len(outs),
            compiler_params=parameters,
        )(*args)

    live_counts = live_counts.T
    other = lax.ppermute(out_grad, "tp", [(0, 1), (1, 0), (2, 3), (3, 2)])
    kv, live, limits = pl.pallas_call(
        start_kernel,
        out_shape=[
            jax.ShapeDtypeStruct((NF, 2 * SLOTS, WIDTH), BF16),
            jax.ShapeDtypeStruct((ROWS, HS), F32),
            jax.ShapeDtypeStruct((2 * NF, HS), jnp.int32),
        ],
        in_specs=[anywhere] * 3,
        out_specs=[anywhere] * 3,
        scratch_shapes=[
            pltpu.SMEM(live_counts.shape, jnp.int32),
            pltpu.VMEM((SLOTS, WIDTH), BF16),
            pltpu.VMEM((SLOTS, WIDTH), BF16),
            pltpu.VMEM((BATCH, 2 * SLOTS, WIDTH), BF16),
            pltpu.VMEM((ROWS, HS), F32),
            pltpu.VMEM((2 * NF, HS), jnp.int32),
            pltpu.SemaphoreType.DMA((3,)),
            pltpu.SemaphoreType.DMA((NF // BATCH + 2,)),
        ],
    )(live_counts, attn_key, attn_value)
    kv = lax.all_to_all(kv, FAR, 0, 0)
    (grad,) = pl.pallas_call(
        pair_kernel,
        out_shape=[jax.ShapeDtypeStruct((2, *out_grad.shape), BF16)],
        in_specs=[vmem] * 2,
        out_specs=[vmem],
        compiler_params=parameters,
        cost_estimate=pl.CostEstimate(flops=10**11, bytes_accessed=10**8, transcendentals=0),
    )(out_grad, other)
    grad = lax.all_gather(grad, "tp", axis=0, tiled=True, axis_index_groups=[[0, 3], [1, 2]])
    (qd,) = run(
        project_kernel, [((ROWS, 2 * WIDTH + MODEL), BF16)], (live, grad, out_weight, attn_query)
    )
    qd = lax.all_gather(qd, NEAR, axis=0, tiled=False)
    kinds = (CAP2, PAD3)
    tables = [(NF * slots, 2 * NEARS * slots) for slots in kinds]
    *ready, columns = run(
        prepare_kernel,
        [
            item
            for table in tables
            for item in (((table[1], WIDTH), BF16), ((table[1], WIDTH), BF16), (table, F32))
        ]
        + [((NF * COLS, QROWS), BF16)],
        (limits, qd),
    )
    stats, *kept = run(
        stats_kernel,
        [((QROWS + STATS, WIDTH), BF16)] + [(table, F32) for table in tables for _ in range(2)],
        (kv, *ready),
    )
    stats = lax.all_gather(stats, NEAR, axis=0, tiled=False)
    back, *dscores = pl.pallas_call(
        grads_kernel,
        out_shape=[jax.ShapeDtypeStruct((NF, BACK, WIDTH), BF16)]
        + [jax.ShapeDtypeStruct(table, BF16) for table in tables],
        in_specs=[vmem] * 10,
        out_specs=[anywhere, vmem, vmem],
        scratch_shapes=[pltpu.VMEM((NF, BACK, WIDTH), BF16), pltpu.SemaphoreType.DMA((NF // PART,))],
        compiler_params=parameters,
    )(stats, *ready[0:2], *ready[3:5], columns, *kept)
    back = lax.all_to_all(back, FAR, 0, 0)
    (dq,) = run(partial_kernel, [((QROWS, WIDTH), F32)], (kv, *dscores))
    dq = lax.all_gather(dq, NEAR, axis=0, tiled=False)
    (query_grad,) = run(query_kernel, [((SLOTS, WIDTH), BF16)], (dq,))
    key_grad, value_grad, weight_grad = run(
        last_kernel,
        [((SLOTS, WIDTH), BF16), ((SLOTS, WIDTH), BF16), ((COLS, WIDTH), F32)],
        (back,),
    )
    return query_grad, key_grad, value_grad, weight_grad.T


def solution(mesh):
    grid = Mesh(mesh.devices.reshape(NZ, NY, NX, NC, TP), ("z", "y", "x", "c", "tp"))
    seq = ("z", "y", "x", "c")
    rows = P(seq, "tp")
    return jax.shard_map(
        on_device,
        mesh=grid,
        in_specs=(P(), P(), rows, rows, rows, rows, P("tp", None)),
        out_specs=(rows, rows, rows, P("tp", seq)),
        check_vma=False,
    )
```

time: 82.2 us -> 80.8 us (0.983)
  blocking collectives: 33.2 us -> 30.3 us
  waiting for transfers between devices: 17.2 us -> 18.9 us
    ppermute x0 -> x1, starting transfers between devices: none -> 5.05 us  [on_device(): other = lax.ppermute(out_grad, 'tp', [(0, 1), (1, 0), (2, 3), (3, 2)])]
    all_to_all x1, starting transfers between devices: 9.49 us -> 5.11 us  [on_device(): back = lax.all_to_all(back, FAR, 0, 0)]
    all_gather x1 -> x0, blocking collectives: 4.25 us -> none  [on_device(): lax.all_gather(out_grad[None], 'tp', axis=0, tiled=True, axis_index_group...]
    all_gather x1, blocking collectives: 5.69 us -> 8.12 us  [on_device(): stats = lax.all_gather(stats, NEAR, axis=0, tiled=False)]
    all_to_all x1, waiting for transfers between devices: 0.01 us -> 1.98 us  [on_device(): kv = lax.all_to_all(kv, FAR, 0, 0)]
    pallas_call x0 -> x2, Pallas kernels: none -> 1.5 us  [the longest x1 1.49 us: on_device(): pl.pallas_call(grads_kernel, out_shape=[jax.ShapeDtypeStruct((NF, BACK, W...]
    pallas_call x5 -> x6, Pallas kernels: 4.36 us -> 3.39 us  [run(): pl.pallas_call(kernel, out_shape=[jax.ShapeDtypeStruct(*o) for o in outs]...]
    all_to_all x1, starting transfers between devices: 13.7 us -> 12.9 us  [on_device(): kv = lax.all_to_all(kv, FAR, 0, 0)]
  transfers between devices with their start and end apart: 2 -> 3, of which waited for: 1 -> 2; matrix products, arithmetic and copies ran while one was open for 0% -> 0% of each run, Pallas kernels for 1% -> 4%
where the time goes in v5:
time: 80.8 us; the launch traced here: 79.6 us
  blocking collectives  30.3 us (38%)
  starting transfers between devices  23.1 us (29%)
  waiting for transfers between devices  18.9 us (23%)
  Pallas kernels  6.55 us (8%)
    all_to_all x1, waiting for transfers between devices, on_device(): back = lax.all_to_all(back, FAR, 0, 0)  16.9 us
    all_to_all x1, starting transfers between devices, on_device(): kv = lax.all_to_all(kv, FAR, 0, 0)  12.9 us
    all_gather x1, blocking collectives, on_device(): qd = lax.all_gather(qd, NEAR, axis=0, tiled=False)  9.43 us
    all_gather x1, blocking collectives, on_device(): stats = lax.all_gather(stats, NEAR, axis=0, tiled=False)  8.12 us
    all_gather x1, blocking collectives, on_device(): dq = lax.all_gather(dq, NEAR, axis=0, tiled=False)  6.58 us
    all_gather x1, blocking collectives, on_device(): lax.all_gather(grad, 'tp', axis=0, tiled=True, axis_index_groups=[[0, 3],...  6.14 us
    all_to_all x1, starting transfers between devices, on_device(): back = lax.all_to_all(back, FAR, 0, 0)  5.11 us
    ppermute x1, starting transfers between devices, on_device(): other = lax.ppermute(out_grad, 'tp', [(0, 1), (1, 0), (2, 3), (3, 2)])  5.05 us
  transfers between devices with their start and end apart: 3, of which 2 were waited for; matrix products, arithmetic and copies ran while one was open for 0% of the time, Pallas kernels for 4%

profile of v5, /device:TPU:1, one launch (start us, length us, event | category | flops | bytes accessed | tf_op | source)
XLA Modules:
  0.0 79.6 jit_solution(6085489207917198821)
XLA Ops:
  0.6 5.0 %collective-permute-start = (bf16[20,512]{1,0:T(8,128)(2,1)}, bf16[20,512]{1,0:T(8,128)(2,1)S(1)}, u32[]{:S(2)}, u32[]{:S(2)}) collective-permute-start(bf16[20,512]{1,0:T(8,128)(2,1)} %own_ref.1), channel_id=1, source_target_pairs={{0,1},{1,0},{2,3},{3,2},{4,5},{5,4},{6,7},{7,6},{8,9},{9,8},{10,11... | collective-permute-start | bytes 61448 | tf_op jit(solution)/shard_map/ppermute | solution.py:316
  5.7 1.7 %shard_map.93 = (bf16[32,40,256]{2,1,0:T(8,128)(2,1)}, f32[24,128]{1,0:T(8,128)}, s32[64,128]{1,0:T(8,128)}) custom-call(s32[2,128]{1,0:T(2,128)} %bitcast.8, bf16[20,256]{1,0:T(8,128)(2,1)} %key_any.1, bf16[20,256]{1,0:T(8,128)(2,1)} %value_any.1), custom_call_target="tpu_custom_call" | custom-call | tf_op jit(solution)/shard_map/pallas_call | solution.py:317
  7.4 0.0 copy-start.4
  7.4 12.9 %all-to-all-start = ((bf16[32,40,256]{2,1,0:T(8,128)(2,1)}), bf16[32,40,256]{2,1,0:T(8,128)(2,1)S(1)}, u32[]{:S(2)}, u32[]{:S(2)}) async-start(bf16[32,40,256]{2,1,0:T(8,128)(2,1)} %get-tuple-element.25), calls=%async_computation | async-start | bytes 1310720 | tf_op jit(solution)/shard_map/all_to_all | solution.py:337
  20.3 0.0 copy-start
  20.3 0.0 collective-permute-done.other_ref
  20.3 0.0 copy-done.4
  20.3 0.0 copy-start.2
  20.3 0.0 copy-start.3
  20.3 6.1 %all_gather.21.grad_ref = bf16[4,20,512]{2,1,0:T(8,128)(2,1)S(1)} all-gather(bf16[2,20,512]{2,1,0:T(8,128)(2,1)S(1)} %shard_map.94), channel_id=1, replica_groups={{0,3},{1,2},{4,7},{5,6},{8,11},{9,10},{12,15},{13,14},{16,19},{17,18},{..., dimensions={0}, use_global_device_ids=true | all-gather | bytes 122880 | tf_op jit(solution)/shard_map/all_gather | solution.py:346
  26.5 0.0 copy-done
  26.5 0.0 copy-done.2
  26.5 0.0 copy-done.3
  26.5 0.4 shard_map.95
  26.9 0.0 copy-start.1
  26.9 9.4 %all-gather = bf16[96,2560]{1,0:T(8,128)(2,1)S(1)} all-gather(bf16[24,2560]{1,0:T(8,128)(2,1)S(1)} %shard_map.95), channel_id=2, replica_groups=mesh['z'=8,'y'=2,'x'=4,'c'=2,'tp'=4] {'y','c'}, dimensions={0}, use_global_device_ids=true | all-gather | bytes 614400 | tf_op jit(solution)/shard_map/all_gather | solution.py:350
  36.4 0.0 copy-done.1
  36.4 0.4 shard_map.96
  36.8 2.0 %all-to-all-done.kv_ref = bf16[32,40,256]{2,1,0:T(8,128)(2,1)S(1)} async-done(((bf16[32,40,256]{2,1,0:T(8,128)(2,1)}), bf16[32,40,256]{2,1,0:T(8,128)(2,1)S(1)}, u32[]{:S(2)}, u32[]{:S(2)}) %all-to-all-start) | async-done | bytes 655392 | tf_op jit(solution)/shard_map/all_to_all | solution.py:337
  38.8 0.9 %shard_map.97 = (bf16[112,256]{1,0:T(8,128)(2,1)S(1)}, f32[512,128]{1,0:T(8,128)S(1)}, f32[512,128]{1,0:T(8,128)S(1)}, f32[256,64]{1,0:T(8,128)S(1)}, f32[256,64]{1,0:T(8,128)S(1)}) custom-call(bf16[32,40,256]{2,1,0:T(8,128)(2,1)S(1)} %all-to-all-done.kv_ref, bf16[128,256]{1,0:T(8,128)(2,1)S(1)} %get-tuple-element.28.refs_0_, ...), custom_call_target="tpu_custom_call" | custom-call | tf_op jit(solution)/shard_map/pallas_call | solution.py:307
  39.8 8.1 %all-gather.1 = bf16[448,256]{1,0:T(8,128)(2,1)S(1)} all-gather(bf16[112,256]{1,0:T(8,128)(2,1)S(1)} %get-tuple-element.34), channel_id=3, replica_groups=mesh['z'=8,'y'=2,'x'=4,'c'=2,'tp'=4] {'y','c'}, dimensions={0}, use_global_device_ids=true | all-gather | bytes 286720 | tf_op jit(solution)/shard_map/all_gather | solution.py:368
  47.9 1.5 %shard_map.98 = (bf16[32,56,256]{2,1,0:T(8,128)(2,1)}, bf16[512,128]{1,0:T(8,128)(2,1)S(1)}, bf16[256,64]{1,0:T(8,128)(2,1)S(1)}) custom-call(bf16[4,112,256]{2,1,0:T(8,128)(2,1)S(1)} %bitcast.7, bf16[128,256]{1,0:T(8,128)(2,1)S(1)} %get-tuple-element.28.refs_0_, bf16[128,256]{1,0:T(8,128)(2,1)S(1)} %get-tuple-element.29.refs_1_, ...), custom_call_target="tpu_custom_call" | custom-call | tf_op jit(solution)/shard_map/pallas_call | solution.py:369
  49.4 5.1 %all-to-all-start.1 = ((bf16[32,56,256]{2,1,0:T(8,128)(2,1)}), bf16[32,56,256]{2,1,0:T(8,128)(2,1)S(1)}, u32[]{:S(2)}, u32[]{:S(2)}) async-start(bf16[32,56,256]{2,1,0:T(8,128)(2,1)} %get-tuple-element.42), calls=%async_computation.1 | async-start | bytes 1835008 | tf_op jit(solution)/shard_map/all_to_all | solution.py:378
  54.5 0.2 shard_map.99
  54.7 6.6 %all-gather.2 = f32[384,256]{1,0:T(8,128)S(1)} all-gather(f32[96,256]{1,0:T(8,128)S(1)} %shard_map.99), channel_id=4, replica_groups=mesh['z'=8,'y'=2,'x'=4,'c'=2,'tp'=4] {'y','c'}, dimensions={0}, use_global_device_ids=true | all-gather | bytes 491520 | tf_op jit(solution)/shard_map/all_gather | solution.py:380
  61.3 0.6 shard_map.100
  61.9 16.9 %all-to-all-done.1.in_ref = bf16[32,56,256]{2,1,0:T(8,128)(2,1)S(1)} async-done(((bf16[32,56,256]{2,1,0:T(8,128)(2,1)}), bf16[32,56,256]{2,1,0:T(8,128)(2,1)S(1)}, u32[]{:S(2)}, u32[]{:S(2)}) %all-to-all-start.1) | async-done | bytes 917536 | tf_op jit(solution)/shard_map/all_to_all | solution.py:378
  78.9 0.7 shard_map.101
  (1 shorter events, 0.0 us)
Async XLA Ops:
  0.6 19.7 %collective-permute-start = (bf16[20,512]{1,0:T(8,128)(2,1)}, bf16[20,512]{1,0:T(8,128)(2,1)S(1)}, u32[]{:S(2)}, u32[]{:S(2)}) collective-permute-start(bf16[20,512]{1,0:T(8,128)(2,1)} %own_ref.1), channel_id=1, source_target_pairs={{0,1},{1,0},{2,3},{3,2},{4,5},{5,4},{6,7},{7,6},{8,9},{9,8},{10,11... | collective-permute-start | bytes 61448 | tf_op jit(solution)/shard_map/ppermute | solution.py:316
  7.4 12.9 %copy-start.4 = (bf16[20,512]{1,0:T(8,128)(2,1)S(1)}, bf16[20,512]{1,0:T(8,128)(2,1)}, u32[]{:S(2)}) copy-start(bf16[20,512]{1,0:T(8,128)(2,1)} %own_ref.1) | copy-start | bytes 61444
  7.4 31.4 %all-to-all-start = ((bf16[32,40,256]{2,1,0:T(8,128)(2,1)}), bf16[32,40,256]{2,1,0:T(8,128)(2,1)S(1)}, u32[]{:S(2)}, u32[]{:S(2)}) async-start(bf16[32,40,256]{2,1,0:T(8,128)(2,1)} %get-tuple-element.25), calls=%async_computation | async-start | bytes 1310720 | tf_op jit(solution)/shard_map/all_to_all | solution.py:337
  20.3 6.2 %copy-start = (bf16[256,2048]{1,0:T(8,128)(2,1)S(1)}, bf16[256,2048]{1,0:T(8,128)(2,1)}, u32[]{:S(2)}) copy-start(bf16[256,2048]{1,0:T(8,128)(2,1)} %weight_ref.1) | copy-start | bytes 3145732
  20.3 6.2 %copy-start.2 = (bf16[20,256]{1,0:T(8,128)(2,1)S(1)}, bf16[20,256]{1,0:T(8,128)(2,1)}, u32[]{:S(2)}) copy-start(bf16[20,256]{1,0:T(8,128)(2,1)} %query_ref.1) | copy-start | bytes 30724
  20.3 6.2 %copy-start.3 = (f32[24,128]{1,0:T(8,128)S(1)}, f32[24,128]{1,0:T(8,128)}, u32[]{:S(2)}) copy-start(f32[24,128]{1,0:T(8,128)} %get-tuple-element.27.live_ref) | copy-start | bytes 36868
  26.9 9.5 %copy-start.1 = (s32[64,128]{1,0:T(8,128)S(1)}, s32[64,128]{1,0:T(8,128)}, u32[]{:S(2)}) copy-start(s32[64,128]{1,0:T(8,128)} %get-tuple-element.26.limit_ref) | copy-start | bytes 98308
  49.4 29.5 %all-to-all-start.1 = ((bf16[32,56,256]{2,1,0:T(8,128)(2,1)}), bf16[32,56,256]{2,1,0:T(8,128)(2,1)S(1)}, u32[]{:S(2)}, u32[]{:S(2)}) async-start(bf16[32,56,256]{2,1,0:T(8,128)(2,1)} %get-tuple-element.42), calls=%async_computation.1 | async-start | bytes 1835008 | tf_op jit(solution)/shard_map/all_to_all | solution.py:378

commit v6 on v5

--- a/solution.py
+++ b/solution.py
@@ -3,13 +3,10 @@
 from jax import lax
 from jax.experimental import pallas as pl
 from jax.experimental.pallas import tpu as pltpu
-from jax.sharding import Mesh
 from jax.sharding import PartitionSpec as P
 
 HS = 128
 NZ, NY, NX, NC = 8, 2, 4, 2
-FAR = ("z", "x")
-NEAR = ("y", "c")
 NF, NEARS = NZ * NX, NY * NC
 TP = 4
 SLOTS = 20
@@ -67,7 +64,26 @@
 
 
 def place():
-    return tuple(lax.axis_index(axis) for axis in ("z", "y", "x", "c"))
+    index = lax.axis_index("seq")
+    return index // (NY * NX * NC), index // (NX * NC) % NY, index // NC % NX, index % NC
+
+
+def far_place(index):
+    return NZ - 1 - index // NX, index % NX
+
+
+def far_groups():
+    return [
+        [shard_of(far_place(f)[0], y, far_place(f)[1], c) for f in range(NF)]
+        for y in range(NY)
+        for c in range(NC)
+    ]
+
+
+def near_groups():
+    return [
+        [shard_of(z, n // NC, x, n % NC) for n in range(NEARS)] for z in range(NZ) for x in range(NX)
+    ]
 
 
 def allowed(limit_ref, which, slots):
@@ -76,7 +92,8 @@
     key_row = lax.broadcasted_iota(jnp.int32, shape, 0)
     query_row = lax.broadcasted_iota(jnp.int32, shape, 1) % (NEARS * slots)
     key_far, key_slot = key_row // slots, key_row % slots
-    key_shard = shard_of(key_far // NX, y, key_far % NX, c)
+    key_z, key_x = far_place(key_far)
+    key_shard = shard_of(key_z, y, key_x, c)
     near, query_slot = query_row // slots, query_row % slots
     query_shard = shard_of(z, near // NC, x, near % NC)
     limit = limit_ref[which * NF : (which + 1) * NF, : shape[1]]
@@ -122,7 +139,8 @@
     live[...] = jnp.where(slot < limit, 1.0, 0.0)
     for which in range(2):
         for f in range(NF):
-            limit = counts[which, shard_of(f // NX, y, f % NX, c)]
+            far_z, far_x = far_place(f)
+            limit = counts[which, shard_of(far_z, y, far_x, c)]
             limits[which * NF + f : which * NF + f + 1, :] = jnp.full((1, HS), limit, jnp.int32)
     rest = [
         pltpu.make_async_copy(live, live_any, out_sems.at[batches]),
@@ -166,7 +184,8 @@
         d_attn_ref[...] = by_head(qd_parts[which][:, WIDTH:])
         bias_ref[...] = jnp.where(allowed(limit_ref, which, slots), 0.0, LOW)
     columns_ref = refs[6]
-    for z in range(NZ):
+    for step in range(NZ):
+        z, _ = far_place(step * NX)
         column = pl.multiple_of(2 * WIDTH + (z * NY + y) * HS, HS)
         wide = qd_ref[:, :, pl.ds(column, HS)].astype(F32)
         rows = jnp.concatenate(
@@ -174,7 +193,7 @@
         )
         down = rows.T.reshape(NX, NC, COLS, QROWS)
         own = jnp.where(c == 0, down[:, 0], down[:, 1]).reshape(NX * COLS, QROWS)
-        columns_ref[z * NX * COLS : (z + 1) * NX * COLS] = own.astype(BF16)
+        columns_ref[step * NX * COLS : (step + 1) * NX * COLS] = own.astype(BF16)
 
 
 def unpacked(kv_ref):
@@ -334,7 +353,7 @@
             pltpu.SemaphoreType.DMA((NF // BATCH + 2,)),
         ],
     )(live_counts, attn_key, attn_value)
-    kv = lax.all_to_all(kv, FAR, 0, 0)
+    kv = lax.all_to_all(kv, "seq", 0, 0, axis_index_groups=far_groups())
     (grad,) = pl.pallas_call(
         pair_kernel,
         out_shape=[jax.ShapeDtypeStruct((2, *out_grad.shape), BF16)],
@@ -347,7 +366,7 @@
     (qd,) = run(
         project_kernel, [((ROWS, 2 * WIDTH + MODEL), BF16)], (live, grad, out_weight, attn_query)
     )
-    qd = lax.all_gather(qd, NEAR, axis=0, tiled=False)
+    qd = lax.all_gather(qd, "seq", axis=0, tiled=False, axis_index_groups=near_groups())
     kinds = (CAP2, PAD3)
     tables = [(NF * slots, 2 * NEARS * slots) for slots in kinds]
     *ready, columns = run(
@@ -365,7 +384,7 @@
         [((QROWS + STATS, WIDTH), BF16)] + [(table, F32) for table in tables for _ in range(2)],
         (kv, *ready),
     )
-    stats = lax.all_gather(stats, NEAR, axis=0, tiled=False)
+    stats = lax.all_gather(stats, "seq", axis=0, tiled=False, axis_index_groups=near_groups())
     back, *dscores = pl.pallas_call(
         grads_kernel,
         out_shape=[jax.ShapeDtypeStruct((NF, BACK, WIDTH), BF16)]
@@ -375,9 +394,9 @@
         scratch_shapes=[pltpu.VMEM((NF, BACK, WIDTH), BF16), pltpu.SemaphoreType.DMA((NF // PART,))],
         compiler_params=parameters,
     )(stats, *ready[0:2], *ready[3:5], columns, *kept)
-    back = lax.all_to_all(back, FAR, 0, 0)
+    back = lax.all_to_all(back, "seq", 0, 0, axis_index_groups=far_groups())
     (dq,) = run(partial_kernel, [((QROWS, WIDTH), F32)], (kv, *dscores))
-    dq = lax.all_gather(dq, NEAR, axis=0, tiled=False)
+    dq = lax.all_gather(dq, "seq", axis=0, tiled=False, axis_index_groups=near_groups())
     (query_grad,) = run(query_kernel, [((SLOTS, WIDTH), BF16)], (dq,))
     key_grad, value_grad, weight_grad = run(
         last_kernel,
@@ -388,13 +407,11 @@
 
 
 def solution(mesh):
-    grid = Mesh(mesh.devices.reshape(NZ, NY, NX, NC, TP), ("z", "y", "x", "c", "tp"))
-    seq = ("z", "y", "x", "c")
-    rows = P(seq, "tp")
+    rows = P("seq", "tp")
     return jax.shard_map(
         on_device,
-        mesh=grid,
+        mesh=mesh,
         in_specs=(P(), P(), rows, rows, rows, rows, P("tp", None)),
-        out_specs=(rows, rows, rows, P("tp", seq)),
+        out_specs=(rows, rows, rows, P("tp", "seq")),
         check_vma=False,
     )

time: 80.8 us -> 78 us (0.965)
  waiting for transfers between devices: 18.9 us -> 14 us
  starting transfers between devices: 23.1 us -> 25.5 us
    all_to_all x2, waiting for transfers between devices: 18.9 us -> 14 us  [the longest x1 14 us: on_device(): back = lax.all_to_all(back, 'seq', 0, 0, axis_index_groups=far_groups())]
    all_to_all x2, starting transfers between devices: 18 us -> 20.5 us  [the longest x1 13 us: on_device(): kv = lax.all_to_all(kv, 'seq', 0, 0, axis_index_groups=far_groups())]
  transfers between devices with their start and end apart: 3 -> 3, of which waited for: 2 -> 1; matrix products, arithmetic and copies ran while one was open for 0% -> 0% of each run, Pallas kernels for 4% -> 4%
where the time goes in v6:
time: 78 us; the launch traced here: 77 us
  blocking collectives  30.1 us (39%)
  starting transfers between devices  25.5 us (33%)
  waiting for transfers between devices  14 us (18%)
  Pallas kernels  6.56 us (8%)
    all_to_all x1, waiting for transfers between devices, on_device(): back = lax.all_to_all(back, 'seq', 0, 0, axis_index_groups=far_groups())  14 us
    all_to_all x1, starting transfers between devices, on_device(): kv = lax.all_to_all(kv, 'seq', 0, 0, axis_index_groups=far_groups())  13 us
    all_gather x1, blocking collectives, on_device(): lax.all_gather(qd, 'seq', axis=0, tiled=False, axis_index_groups=near_gro...  9.7 us
    all_gather x1, blocking collectives, on_device(): lax.all_gather(stats, 'seq', axis=0, tiled=False, axis_index_groups=near_...  7.46 us
    all_to_all x1, starting transfers between devices, on_device(): back = lax.all_to_all(back, 'seq', 0, 0, axis_index_groups=far_groups())  7.46 us
    all_gather x1, blocking collectives, on_device(): lax.all_gather(dq, 'seq', axis=0, tiled=False, axis_index_groups=near_gro...  6.75 us
    all_gather x1, blocking collectives, on_device(): lax.all_gather(grad, 'tp', axis=0, tiled=True, axis_index_groups=[[0, 3],...  6.15 us
    ppermute x1, starting transfers between devices, on_device(): other = lax.ppermute(out_grad, 'tp', [(0, 1), (1, 0), (2, 3), (3, 2)])  5.05 us
  transfers between devices with their start and end apart: 3, of which 1 were waited for; matrix products, arithmetic and copies ran while one was open for 0% of the time, Pallas kernels for 4%

profile of v6, /device:TPU:1, one launch (start us, length us, event | category | flops | bytes accessed | tf_op | source)
XLA Modules:
  0.0 77.0 jit_solution(11206086043442385010)
XLA Ops:
  0.6 5.0 %collective-permute-start = (bf16[20,512]{1,0:T(8,128)(2,1)}, bf16[20,512]{1,0:T(8,128)(2,1)S(1)}, u32[]{:S(2)}, u32[]{:S(2)}) collective-permute-start(bf16[20,512]{1,0:T(8,128)(2,1)} %own_ref.1), channel_id=1, source_target_pairs={{0,1},{1,0},{2,3},{3,2},{4,5},{5,4},{6,7},{7,6},{8,9},{9,8},{10,11... | collective-permute-start | bytes 61448 | tf_op jit(solution)/shard_map/ppermute | solution.py:335
  5.7 1.7 %shard_map.93 = (bf16[32,40,256]{2,1,0:T(8,128)(2,1)}, f32[24,128]{1,0:T(8,128)}, s32[64,128]{1,0:T(8,128)}) custom-call(s32[2,128]{1,0:T(2,128)} %bitcast.8, bf16[20,256]{1,0:T(8,128)(2,1)} %key_any.1, bf16[20,256]{1,0:T(8,128)(2,1)} %value_any.1), custom_call_target="tpu_custom_call" | custom-call | tf_op jit(solution)/shard_map/pallas_call | solution.py:336
  7.4 0.0 copy-start.4
  7.4 13.0 %all-to-all-start = ((bf16[32,40,256]{2,1,0:T(8,128)(2,1)}), bf16[32,40,256]{2,1,0:T(8,128)(2,1)S(1)}, u32[]{:S(2)}, u32[]{:S(2)}) async-start(bf16[32,40,256]{2,1,0:T(8,128)(2,1)} %get-tuple-element.25), calls=%async_computation | async-start | bytes 1310720 | tf_op jit(solution)/shard_map/all_to_all | solution.py:356
  20.4 0.0 copy-start
  20.4 0.0 collective-permute-done.other_ref
  20.4 0.0 copy-done.4
  20.4 0.0 copy-start.2
  20.5 0.0 copy-start.3
  20.5 6.2 %all_gather.21.grad_ref = bf16[4,20,512]{2,1,0:T(8,128)(2,1)S(1)} all-gather(bf16[2,20,512]{2,1,0:T(8,128)(2,1)S(1)} %shard_map.94), channel_id=1, replica_groups={{0,3},{1,2},{4,7},{5,6},{8,11},{9,10},{12,15},{13,14},{16,19},{17,18},{..., dimensions={0}, use_global_device_ids=true | all-gather | bytes 122880 | tf_op jit(solution)/shard_map/all_gather | solution.py:365
  26.6 0.0 copy-done
  26.6 0.0 copy-done.2
  26.6 0.0 copy-done.3
  26.6 0.4 shard_map.95
  27.0 0.0 copy-start.1
  27.1 9.7 %all-gather = bf16[96,2560]{1,0:T(8,128)(2,1)S(1)} all-gather(bf16[24,2560]{1,0:T(8,128)(2,1)S(1)} %shard_map.95), channel_id=2, replica_groups={{0,4,32,36},{8,12,40,44},{16,20,48,52},{24,28,56,60},{64,68,96,100},{72..., dimensions={0}, use_global_device_ids=true | all-gather | bytes 614400 | tf_op jit(solution)/shard_map/all_gather | solution.py:369
  36.8 0.0 copy-done.1
  36.8 0.5 shard_map.96
  37.2 0.0 all-to-all-done.kv_ref
  37.2 0.9 %shard_map.97 = (bf16[112,256]{1,0:T(8,128)(2,1)S(1)}, f32[512,128]{1,0:T(8,128)S(1)}, f32[512,128]{1,0:T(8,128)S(1)}, f32[256,64]{1,0:T(8,128)S(1)}, f32[256,64]{1,0:T(8,128)S(1)}) custom-call(bf16[32,40,256]{2,1,0:T(8,128)(2,1)S(1)} %all-to-all-done.kv_ref, bf16[128,256]{1,0:T(8,128)(2,1)S(1)} %get-tuple-element.28.refs_0_, ...), custom_call_target="tpu_custom_call" | custom-call | tf_op jit(solution)/shard_map/pallas_call | solution.py:326
  38.2 7.5 %all-gather.1 = bf16[448,256]{1,0:T(8,128)(2,1)S(1)} all-gather(bf16[112,256]{1,0:T(8,128)(2,1)S(1)} %get-tuple-element.34), channel_id=3, replica_groups={{0,4,32,36},{8,12,40,44},{16,20,48,52},{24,28,56,60},{64,68,96,100},{72..., dimensions={0}, use_global_device_ids=true | all-gather | bytes 286720 | tf_op jit(solution)/shard_map/all_gather | solution.py:387
  45.7 1.5 %shard_map.98 = (bf16[32,56,256]{2,1,0:T(8,128)(2,1)}, bf16[512,128]{1,0:T(8,128)(2,1)S(1)}, bf16[256,64]{1,0:T(8,128)(2,1)S(1)}) custom-call(bf16[4,112,256]{2,1,0:T(8,128)(2,1)S(1)} %bitcast.7, bf16[128,256]{1,0:T(8,128)(2,1)S(1)} %get-tuple-element.28.refs_0_, bf16[128,256]{1,0:T(8,128)(2,1)S(1)} %get-tuple-element.29.refs_1_, ...), custom_call_target="tpu_custom_call" | custom-call | tf_op jit(solution)/shard_map/pallas_call | solution.py:388
  47.2 7.5 %all-to-all-start.1 = ((bf16[32,56,256]{2,1,0:T(8,128)(2,1)}), bf16[32,56,256]{2,1,0:T(8,128)(2,1)S(1)}, u32[]{:S(2)}, u32[]{:S(2)}) async-start(bf16[32,56,256]{2,1,0:T(8,128)(2,1)} %get-tuple-element.42), calls=%async_computation.1 | async-start | bytes 1835008 | tf_op jit(solution)/shard_map/all_to_all | solution.py:397
  54.6 0.2 shard_map.99
  54.9 6.7 %all-gather.2 = f32[384,256]{1,0:T(8,128)S(1)} all-gather(f32[96,256]{1,0:T(8,128)S(1)} %shard_map.99), channel_id=4, replica_groups={{0,4,32,36},{8,12,40,44},{16,20,48,52},{24,28,56,60},{64,68,96,100},{72..., dimensions={0}, use_global_device_ids=true | all-gather | bytes 491520 | tf_op jit(solution)/shard_map/all_gather | solution.py:399
  61.6 0.6 shard_map.100
  62.2 14.0 %all-to-all-done.1.in_ref = bf16[32,56,256]{2,1,0:T(8,128)(2,1)S(1)} async-done(((bf16[32,56,256]{2,1,0:T(8,128)(2,1)}), bf16[32,56,256]{2,1,0:T(8,128)(2,1)S(1)}, u32[]{:S(2)}, u32[]{:S(2)}) %all-to-all-start.1) | async-done | bytes 917536 | tf_op jit(solution)/shard_map/all_to_all | solution.py:397
  76.3 0.7 shard_map.101
  (1 shorter events, 0.0 us)
Async XLA Ops:
  0.6 19.8 %collective-permute-start = (bf16[20,512]{1,0:T(8,128)(2,1)}, bf16[20,512]{1,0:T(8,128)(2,1)S(1)}, u32[]{:S(2)}, u32[]{:S(2)}) collective-permute-start(bf16[20,512]{1,0:T(8,128)(2,1)} %own_ref.1), channel_id=1, source_target_pairs={{0,1},{1,0},{2,3},{3,2},{4,5},{5,4},{6,7},{7,6},{8,9},{9,8},{10,11... | collective-permute-start | bytes 61448 | tf_op jit(solution)/shard_map/ppermute | solution.py:335
  7.4 13.1 %copy-start.4 = (bf16[20,512]{1,0:T(8,128)(2,1)S(1)}, bf16[20,512]{1,0:T(8,128)(2,1)}, u32[]{:S(2)}) copy-start(bf16[20,512]{1,0:T(8,128)(2,1)} %own_ref.1) | copy-start | bytes 61444
  7.4 29.9 %all-to-all-start = ((bf16[32,40,256]{2,1,0:T(8,128)(2,1)}), bf16[32,40,256]{2,1,0:T(8,128)(2,1)S(1)}, u32[]{:S(2)}, u32[]{:S(2)}) async-start(bf16[32,40,256]{2,1,0:T(8,128)(2,1)} %get-tuple-element.25), calls=%async_computation | async-start | bytes 1310720 | tf_op jit(solution)/shard_map/all_to_all | solution.py:356
  20.4 6.2 %copy-start = (bf16[256,2048]{1,0:T(8,128)(2,1)S(1)}, bf16[256,2048]{1,0:T(8,128)(2,1)}, u32[]{:S(2)}) copy-start(bf16[256,2048]{1,0:T(8,128)(2,1)} %weight_ref.1) | copy-start | bytes 3145732
  20.4 6.2 %copy-start.2 = (bf16[20,256]{1,0:T(8,128)(2,1)S(1)}, bf16[20,256]{1,0:T(8,128)(2,1)}, u32[]{:S(2)}) copy-start(bf16[20,256]{1,0:T(8,128)(2,1)} %query_ref.1) | copy-start | bytes 30724
  20.5 6.2 %copy-start.3 = (f32[24,128]{1,0:T(8,128)S(1)}, f32[24,128]{1,0:T(8,128)}, u32[]{:S(2)}) copy-start(f32[24,128]{1,0:T(8,128)} %get-tuple-element.27.live_ref) | copy-start | bytes 36868
  27.0 9.7 %copy-start.1 = (s32[64,128]{1,0:T(8,128)S(1)}, s32[64,128]{1,0:T(8,128)}, u32[]{:S(2)}) copy-start(s32[64,128]{1,0:T(8,128)} %get-tuple-element.26.limit_ref) | copy-start | bytes 98308
  47.2 29.1 %all-to-all-start.1 = ((bf16[32,56,256]{2,1,0:T(8,128)(2,1)}), bf16[32,56,256]{2,1,0:T(8,128)(2,1)S(1)}, u32[]{:S(2)}, u32[]{:S(2)}) async-start(bf16[32,56,256]{2,1,0:T(8,128)(2,1)} %get-tuple-element.42), calls=%async_computation.1 | async-start | bytes 1835008 | tf_op jit(solution)/shard_map/all_to_all | solution.py:397

commit v7 on v6

--- a/solution.py
+++ b/solution.py
@@ -22,6 +22,8 @@
 PIECES = 3
 STATS = 16
 PART = 8
+Z_ORDER = (7, 0, 1, 2, 3, 4, 5, 6)
+BACK_ORDER = (0, 1, 2, 3, 28, 29, 30, 31, 24, 25, 26, 27, 20, 21, 22, 23, 16, 17, 18, 19, 12, 13, 14, 15, 8, 9, 10, 11, 4, 5, 6, 7)
 BATCH = 8
 SCALE = HS**-0.5
 LOW = -1e30
@@ -69,12 +71,13 @@
 
 
 def far_place(index):
-    return NZ - 1 - index // NX, index % NX
-
-
-def far_groups():
+    step = index // NX
+    return sum((step == i) * z for i, z in enumerate(Z_ORDER)), index % NX
+
+
+def far_groups(order):
     return [
-        [shard_of(far_place(f)[0], y, far_place(f)[1], c) for f in range(NF)]
+        [shard_of(far_place(f)[0], y, far_place(f)[1], c) for f in order]
         for y in range(NY)
         for c in range(NC)
     ]
@@ -260,27 +263,27 @@
         start += count
     attended = jnp.concatenate(attended, axis=0).astype(BF16)
 
+    for which, slots in ((0, CAP2), (1, PAD3)):
+        query, d_attn = (ref[...] for ref in ready[2 * which : 2 * which + 2])
+        log_total, delta = totals[which]
+        prob = jnp.exp(kept[2 * which][...] - log_total)
+        dscore = (prob * (kept[2 * which + 1][...] - delta)).astype(BF16)
+        dscore_refs[which][...] = dscore
+        d_key = (mm(dscore, query, NN) * SCALE).reshape(NF, slots, WIDTH)
+        d_value = mm(prob.astype(BF16), d_attn, NN).reshape(NF, slots, WIDTH)
+        if which == 0:
+            for message, f in enumerate(BACK_ORDER):
+                block[message, :CAP2] = d_key[f].astype(BF16)
+                block[message, CAP2 : 2 * CAP2] = d_value[f].astype(BF16)
+        else:
+            third = jnp.concatenate([d_key[:, :CAP3], d_value[:, :CAP3]], axis=1)
+    own = mm(columns_ref[...], attended, NN).reshape(NF, COLS, WIDTH)
+    third = jnp.concatenate([third, own], axis=1).astype(BF16)
     sends = []
     for i in range(NF // PART):
+        for message in range(i * PART, (i + 1) * PART):
+            block[message, 2 * CAP2 :] = third[BACK_ORDER[message]]
         parts = slice(i * PART, (i + 1) * PART)
-        third = []
-        for which, slots in ((0, CAP2), (1, PAD3)):
-            query, d_attn = (ref[...] for ref in ready[2 * which : 2 * which + 2])
-            log_total, delta = totals[which]
-            keys = slice(i * PART * slots, (i + 1) * PART * slots)
-            prob = jnp.exp(kept[2 * which][keys] - log_total)
-            dscore = (prob * (kept[2 * which + 1][keys] - delta)).astype(BF16)
-            dscore_refs[which][keys] = dscore
-            d_key = (mm(dscore, query, NN) * SCALE).reshape(PART, slots, WIDTH)
-            d_value = mm(prob.astype(BF16), d_attn, NN).reshape(PART, slots, WIDTH)
-            if which == 0:
-                block[parts, :CAP2] = d_key.astype(BF16)
-                block[parts, CAP2 : 2 * CAP2] = d_value.astype(BF16)
-            else:
-                third = [d_key[:, :CAP3], d_value[:, :CAP3]]
-        columns = columns_ref[i * PART * COLS : (i + 1) * PART * COLS]
-        own = mm(columns, attended, NN).reshape(PART, COLS, WIDTH)
-        block[parts, 2 * CAP2 :] = jnp.concatenate([*third, own], axis=1).astype(BF16)
         sends.append(pltpu.make_async_copy(block.at[parts], out_any.at[parts], sems.at[i]))
         sends[-1].start()
     for send in sends:
@@ -353,7 +356,7 @@
             pltpu.SemaphoreType.DMA((NF // BATCH + 2,)),
         ],
     )(live_counts, attn_key, attn_value)
-    kv = lax.all_to_all(kv, "seq", 0, 0, axis_index_groups=far_groups())
+    kv = lax.all_to_all(kv, "seq", 0, 0, axis_index_groups=far_groups(range(NF)))
     (grad,) = pl.pallas_call(
         pair_kernel,
         out_shape=[jax.ShapeDtypeStruct((2, *out_grad.shape), BF16)],
@@ -394,7 +397,7 @@
         scratch_shapes=[pltpu.VMEM((NF, BACK, WIDTH), BF16), pltpu.SemaphoreType.DMA((NF // PART,))],
         compiler_params=parameters,
     )(stats, *ready[0:2], *ready[3:5], columns, *kept)
-    back = lax.all_to_all(back, "seq", 0, 0, axis_index_groups=far_groups())
+    back = lax.all_to_all(back, "seq", 0, 0, axis_index_groups=far_groups(BACK_ORDER))
     (dq,) = run(partial_kernel, [((QROWS, WIDTH), F32)], (kv, *dscores))
     dq = lax.all_gather(dq, "seq", axis=0, tiled=False, axis_index_groups=near_groups())
     (query_grad,) = run(query_kernel, [((SLOTS, WIDTH), BF16)], (dq,))

time: 78 us -> 77.9 us (level)
  no operation moved by 1% of the time
where the time goes in v7:
time: 77.9 us; the launch traced here: 77.1 us
  blocking collectives  30.8 us (40%)
  starting transfers between devices  24.8 us (32%)
  waiting for transfers between devices  14.1 us (18%)
  Pallas kernels  6.63 us (9%)
    all_to_all x1, waiting for transfers between devices, on_device(): lax.all_to_all(back, 'seq', 0, 0, axis_index_groups=far_groups(BACK_ORDER))  14.1 us
    all_to_all x1, starting transfers between devices, on_device(): lax.all_to_all(kv, 'seq', 0, 0, axis_index_groups=far_groups(range(NF)))  12.9 us
    all_gather x1, blocking collectives, on_device(): lax.all_gather(qd, 'seq', axis=0, tiled=False, axis_index_groups=near_gro...  9.7 us
    all_gather x1, blocking collectives, on_device(): lax.all_gather(stats, 'seq', axis=0, tiled=False, axis_index_groups=near_...  8.21 us
    all_to_all x1, starting transfers between devices, on_device(): lax.all_to_all(back, 'seq', 0, 0, axis_index_groups=far_groups(BACK_ORDER))  6.79 us
    all_gather x1, blocking collectives, on_device(): lax.all_gather(dq, 'seq', axis=0, tiled=False, axis_index_groups=near_gro...  6.71 us
    all_gather x1, blocking collectives, on_device(): lax.all_gather(grad, 'tp', axis=0, tiled=True, axis_index_groups=[[0, 3],...  6.15 us
    ppermute x1, starting transfers between devices, on_device(): other = lax.ppermute(out_grad, 'tp', [(0, 1), (1, 0), (2, 3), (3, 2)])  5.05 us
  transfers between devices with their start and end apart: 3, of which 1 were waited for; matrix products, arithmetic and copies ran while one was open for 0% of the time, Pallas kernels for 4%

profile of v7, /device:TPU:1, one launch (start us, length us, event | category | flops | bytes accessed | tf_op | source)
XLA Modules:
  0.0 77.1 jit_solution(10373892241595845195)
XLA Ops:
  0.6 5.0 %collective-permute-start = (bf16[20,512]{1,0:T(8,128)(2,1)}, bf16[20,512]{1,0:T(8,128)(2,1)S(1)}, u32[]{:S(2)}, u32[]{:S(2)}) collective-permute-start(bf16[20,512]{1,0:T(8,128)(2,1)} %own_ref.1), channel_id=1, source_target_pairs={{0,1},{1,0},{2,3},{3,2},{4,5},{5,4},{6,7},{7,6},{8,9},{9,8},{10,11... | collective-permute-start | bytes 61448 | tf_op jit(solution)/shard_map/ppermute | solution.py:338
  5.7 1.7 %shard_map.93 = (bf16[32,40,256]{2,1,0:T(8,128)(2,1)}, f32[24,128]{1,0:T(8,128)}, s32[64,128]{1,0:T(8,128)}) custom-call(s32[2,128]{1,0:T(2,128)} %bitcast.8, bf16[20,256]{1,0:T(8,128)(2,1)} %key_any.1, bf16[20,256]{1,0:T(8,128)(2,1)} %value_any.1), custom_call_target="tpu_custom_call" | custom-call | tf_op jit(solution)/shard_map/pallas_call | solution.py:339
  7.4 0.0 copy-start.4
  7.4 12.9 %all-to-all-start = ((bf16[32,40,256]{2,1,0:T(8,128)(2,1)}), bf16[32,40,256]{2,1,0:T(8,128)(2,1)S(1)}, u32[]{:S(2)}, u32[]{:S(2)}) async-start(bf16[32,40,256]{2,1,0:T(8,128)(2,1)} %get-tuple-element.25), calls=%async_computation | async-start | bytes 1310720 | tf_op jit(solution)/shard_map/all_to_all | solution.py:359
  20.3 0.0 copy-start
  20.3 0.0 collective-permute-done.other_ref
  20.3 0.0 copy-done.4
  20.4 0.0 copy-start.2
  20.4 0.0 copy-start.3
  20.4 6.2 %all_gather.21.grad_ref = bf16[4,20,512]{2,1,0:T(8,128)(2,1)S(1)} all-gather(bf16[2,20,512]{2,1,0:T(8,128)(2,1)S(1)} %shard_map.94), channel_id=1, replica_groups={{0,3},{1,2},{4,7},{5,6},{8,11},{9,10},{12,15},{13,14},{16,19},{17,18},{..., dimensions={0}, use_global_device_ids=true | all-gather | bytes 122880 | tf_op jit(solution)/shard_map/all_gather | solution.py:368
  26.6 0.0 copy-done
  26.6 0.0 copy-done.2
  26.6 0.0 copy-done.3
  26.6 0.4 shard_map.95
  27.0 0.0 copy-start.1
  27.0 9.7 %all-gather = bf16[96,2560]{1,0:T(8,128)(2,1)S(1)} all-gather(bf16[24,2560]{1,0:T(8,128)(2,1)S(1)} %shard_map.95), channel_id=2, replica_groups={{0,4,32,36},{8,12,40,44},{16,20,48,52},{24,28,56,60},{64,68,96,100},{72..., dimensions={0}, use_global_device_ids=true | all-gather | bytes 614400 | tf_op jit(solution)/shard_map/all_gather | solution.py:372
  36.7 0.0 copy-done.1
  36.7 0.4 shard_map.96
  37.1 0.0 all-to-all-done.kv_ref
  37.1 1.0 %shard_map.97 = (bf16[112,256]{1,0:T(8,128)(2,1)S(1)}, f32[512,128]{1,0:T(8,128)S(1)}, f32[512,128]{1,0:T(8,128)S(1)}, f32[256,64]{1,0:T(8,128)S(1)}, f32[256,64]{1,0:T(8,128)S(1)}) custom-call(bf16[32,40,256]{2,1,0:T(8,128)(2,1)S(1)} %all-to-all-done.kv_ref, bf16[128,256]{1,0:T(8,128)(2,1)S(1)} %get-tuple-element.28.refs_0_, ...), custom_call_target="tpu_custom_call" | custom-call | tf_op jit(solution)/shard_map/pallas_call | solution.py:329
  38.1 8.2 %all-gather.1 = bf16[448,256]{1,0:T(8,128)(2,1)S(1)} all-gather(bf16[112,256]{1,0:T(8,128)(2,1)S(1)} %get-tuple-element.34), channel_id=3, replica_groups={{0,4,32,36},{8,12,40,44},{16,20,48,52},{24,28,56,60},{64,68,96,100},{72..., dimensions={0}, use_global_device_ids=true | all-gather | bytes 286720 | tf_op jit(solution)/shard_map/all_gather | solution.py:390
  46.3 1.6 %shard_map.98 = (bf16[32,56,256]{2,1,0:T(8,128)(2,1)}, bf16[512,128]{1,0:T(8,128)(2,1)S(1)}, bf16[256,64]{1,0:T(8,128)(2,1)S(1)}) custom-call(bf16[4,112,256]{2,1,0:T(8,128)(2,1)S(1)} %bitcast.7, bf16[128,256]{1,0:T(8,128)(2,1)S(1)} %get-tuple-element.28.refs_0_, bf16[128,256]{1,0:T(8,128)(2,1)S(1)} %get-tuple-element.29.refs_1_, ...), custom_call_target="tpu_custom_call" | custom-call | tf_op jit(solution)/shard_map/pallas_call | solution.py:391
  47.9 6.8 %all-to-all-start.1 = ((bf16[32,56,256]{2,1,0:T(8,128)(2,1)}), bf16[32,56,256]{2,1,0:T(8,128)(2,1)S(1)}, u32[]{:S(2)}, u32[]{:S(2)}) async-start(bf16[32,56,256]{2,1,0:T(8,128)(2,1)} %get-tuple-element.42), calls=%async_computation.1 | async-start | bytes 1835008 | tf_op jit(solution)/shard_map/all_to_all | solution.py:400
  54.7 0.2 shard_map.99
  54.9 6.7 %all-gather.2 = f32[384,256]{1,0:T(8,128)S(1)} all-gather(f32[96,256]{1,0:T(8,128)S(1)} %shard_map.99), channel_id=4, replica_groups={{0,4,32,36},{8,12,40,44},{16,20,48,52},{24,28,56,60},{64,68,96,100},{72..., dimensions={0}, use_global_device_ids=true | all-gather | bytes 491520 | tf_op jit(solution)/shard_map/all_gather | solution.py:402
  61.6 0.6 shard_map.100
  62.2 14.1 %all-to-all-done.1.in_ref = bf16[32,56,256]{2,1,0:T(8,128)(2,1)S(1)} async-done(((bf16[32,56,256]{2,1,0:T(8,128)(2,1)}), bf16[32,56,256]{2,1,0:T(8,128)(2,1)S(1)}, u32[]{:S(2)}, u32[]{:S(2)}) %all-to-all-start.1) | async-done | bytes 917536 | tf_op jit(solution)/shard_map/all_to_all | solution.py:400
  76.3 0.7 shard_map.101
  (1 shorter events, 0.0 us)
Async XLA Ops:
  0.6 19.7 %collective-permute-start = (bf16[20,512]{1,0:T(8,128)(2,1)}, bf16[20,512]{1,0:T(8,128)(2,1)S(1)}, u32[]{:S(2)}, u32[]{:S(2)}) collective-permute-start(bf16[20,512]{1,0:T(8,128)(2,1)} %own_ref.1), channel_id=1, source_target_pairs={{0,1},{1,0},{2,3},{3,2},{4,5},{5,4},{6,7},{7,6},{8,9},{9,8},{10,11... | collective-permute-start | bytes 61448 | tf_op jit(solution)/shard_map/ppermute | solution.py:338
  7.4 13.0 %copy-start.4 = (bf16[20,512]{1,0:T(8,128)(2,1)S(1)}, bf16[20,512]{1,0:T(8,128)(2,1)}, u32[]{:S(2)}) copy-start(bf16[20,512]{1,0:T(8,128)(2,1)} %own_ref.1) | copy-start | bytes 61444
  7.4 29.7 %all-to-all-start = ((bf16[32,40,256]{2,1,0:T(8,128)(2,1)}), bf16[32,40,256]{2,1,0:T(8,128)(2,1)S(1)}, u32[]{:S(2)}, u32[]{:S(2)}) async-start(bf16[32,40,256]{2,1,0:T(8,128)(2,1)} %get-tuple-element.25), calls=%async_computation | async-start | bytes 1310720 | tf_op jit(solution)/shard_map/all_to_all | solution.py:359
  20.3 6.2 %copy-start = (bf16[256,2048]{1,0:T(8,128)(2,1)S(1)}, bf16[256,2048]{1,0:T(8,128)(2,1)}, u32[]{:S(2)}) copy-start(bf16[256,2048]{1,0:T(8,128)(2,1)} %weight_ref.1) | copy-start | bytes 3145732
  20.4 6.2 %copy-start.2 = (bf16[20,256]{1,0:T(8,128)(2,1)S(1)}, bf16[20,256]{1,0:T(8,128)(2,1)}, u32[]{:S(2)}) copy-start(bf16[20,256]{1,0:T(8,128)(2,1)} %query_ref.1) | copy-start | bytes 30724
  20.4 6.2 %copy-start.3 = (f32[24,128]{1,0:T(8,128)S(1)}, f32[24,128]{1,0:T(8,128)}, u32[]{:S(2)}) copy-start(f32[24,128]{1,0:T(8,128)} %get-tuple-element.27.live_ref) | copy-start | bytes 36868
  27.0 9.7 %copy-start.1 = (s32[64,128]{1,0:T(8,128)S(1)}, s32[64,128]{1,0:T(8,128)}, u32[]{:S(2)}) copy-start(s32[64,128]{1,0:T(8,128)} %get-tuple-element.26.limit_ref) | copy-start | bytes 98308
  47.9 28.4 %all-to-all-start.1 = ((bf16[32,56,256]{2,1,0:T(8,128)(2,1)}), bf16[32,56,256]{2,1,0:T(8,128)(2,1)S(1)}, u32[]{:S(2)}, u32[]{:S(2)}) async-start(bf16[32,56,256]{2,1,0:T(8,128)(2,1)} %get-tuple-element.42), calls=%async_computation.1 | async-start | bytes 1835008 | tf_op jit(solution)/shard_map/all_to_all | solution.py:400

commit v8 on v6

--- a/solution.py
+++ b/solution.py
@@ -21,7 +21,7 @@
 BACK = 2 * CAP2 + PAD3 + COLS
 PIECES = 3
 STATS = 16
-PART = 8
+PART = 4
 BATCH = 8
 SCALE = HS**-0.5
 LOW = -1e30
@@ -69,12 +69,18 @@
 
 
 def far_place(index):
-    return NZ - 1 - index // NX, index % NX
-
-
-def far_groups():
+    step = index // NX
+    return step - 1 + NZ * (step == 0), index % NX
+
+
+def message_of(index):
+    z, x = far_place(index)
+    return (NZ - 1 - z) * NX + x
+
+
+def far_groups(order):
     return [
-        [shard_of(far_place(f)[0], y, far_place(f)[1], c) for f in range(NF)]
+        [shard_of(far_place(f)[0], y, far_place(f)[1], c) for f in order]
         for y in range(NY)
         for c in range(NC)
     ]
@@ -262,7 +268,8 @@
 
     sends = []
     for i in range(NF // PART):
-        parts = slice(i * PART, (i + 1) * PART)
+        first = message_of(i * PART)
+        parts = slice(first, first + PART)
         third = []
         for which, slots in ((0, CAP2), (1, PAD3)):
             query, d_attn = (ref[...] for ref in ready[2 * which : 2 * which + 2])
@@ -353,7 +360,7 @@
             pltpu.SemaphoreType.DMA((NF // BATCH + 2,)),
         ],
     )(live_counts, attn_key, attn_value)
-    kv = lax.all_to_all(kv, "seq", 0, 0, axis_index_groups=far_groups())
+    kv = lax.all_to_all(kv, "seq", 0, 0, axis_index_groups=far_groups(range(NF)))
     (grad,) = pl.pallas_call(
         pair_kernel,
         out_shape=[jax.ShapeDtypeStruct((2, *out_grad.shape), BF16)],
@@ -394,7 +401,9 @@
         scratch_shapes=[pltpu.VMEM((NF, BACK, WIDTH), BF16), pltpu.SemaphoreType.DMA((NF // PART,))],
         compiler_params=parameters,
     )(stats, *ready[0:2], *ready[3:5], columns, *kept)
-    back = lax.all_to_all(back, "seq", 0, 0, axis_index_groups=far_groups())
+    back = lax.all_to_all(
+        back, "seq", 0, 0, axis_index_groups=far_groups(sorted(range(NF), key=message_of))
+    )
     (dq,) = run(partial_kernel, [((QROWS, WIDTH), F32)], (kv, *dscores))
     dq = lax.all_gather(dq, "seq", axis=0, tiled=False, axis_index_groups=near_groups())
     (query_grad,) = run(query_kernel, [((SLOTS, WIDTH), BF16)], (dq,))

time: 78 us -> 77.9 us (level)
  no operation moved by 1% of the time
where the time goes in v8:
time: 77.9 us; the launch traced here: 77.1 us
  blocking collectives  30.7 us (39%)
  starting transfers between devices  24.8 us (32%)
  waiting for transfers between devices  14.1 us (18%)
  Pallas kernels  6.64 us (9%)
    all_to_all x1, waiting for transfers between devices, on_device(): lax.all_to_all(back, 'seq', 0, 0, axis_index_groups=far_groups(sorted(ran...  14.1 us
    all_to_all x1, starting transfers between devices, on_device(): lax.all_to_all(kv, 'seq', 0, 0, axis_index_groups=far_groups(range(NF)))  12.9 us
    all_gather x1, blocking collectives, on_device(): lax.all_gather(qd, 'seq', axis=0, tiled=False, axis_index_groups=near_gro...  9.7 us
    all_gather x1, blocking collectives, on_device(): lax.all_gather(stats, 'seq', axis=0, tiled=False, axis_index_groups=near_...  8.15 us
    all_to_all x1, starting transfers between devices, on_device(): lax.all_to_all(back, 'seq', 0, 0, axis_index_groups=far_groups(sorted(ran...  6.84 us
    all_gather x1, blocking collectives, on_device(): lax.all_gather(dq, 'seq', axis=0, tiled=False, axis_index_groups=near_gro...  6.71 us
    all_gather x1, blocking collectives, on_device(): lax.all_gather(grad, 'tp', axis=0, tiled=True, axis_index_groups=[[0, 3],...  6.15 us
    ppermute x1, starting transfers between devices, on_device(): other = lax.ppermute(out_grad, 'tp', [(0, 1), (1, 0), (2, 3), (3, 2)])  5.05 us
  transfers between devices with their start and end apart: 3, of which 1 were waited for; matrix products, arithmetic and copies ran while one was open for 0% of the time, Pallas kernels for 4%

profile of v8, /device:TPU:1, one launch (start us, length us, event | category | flops | bytes accessed | tf_op | source)
XLA Modules:
  0.0 77.1 jit_solution(1696404425262896184)
XLA Ops:
  0.6 5.0 %collective-permute-start = (bf16[20,512]{1,0:T(8,128)(2,1)}, bf16[20,512]{1,0:T(8,128)(2,1)S(1)}, u32[]{:S(2)}, u32[]{:S(2)}) collective-permute-start(bf16[20,512]{1,0:T(8,128)(2,1)} %own_ref.1), channel_id=1, source_target_pairs={{0,1},{1,0},{2,3},{3,2},{4,5},{5,4},{6,7},{7,6},{8,9},{9,8},{10,11... | collective-permute-start | bytes 61448 | tf_op jit(solution)/shard_map/ppermute | solution.py:342
  5.7 1.7 %shard_map.93 = (bf16[32,40,256]{2,1,0:T(8,128)(2,1)}, f32[24,128]{1,0:T(8,128)}, s32[64,128]{1,0:T(8,128)}) custom-call(s32[2,128]{1,0:T(2,128)} %bitcast.8, bf16[20,256]{1,0:T(8,128)(2,1)} %key_any.1, bf16[20,256]{1,0:T(8,128)(2,1)} %value_any.1), custom_call_target="tpu_custom_call" | custom-call | tf_op jit(solution)/shard_map/pallas_call | solution.py:343
  7.4 0.0 copy-start.4
  7.4 12.9 %all-to-all-start = ((bf16[32,40,256]{2,1,0:T(8,128)(2,1)}), bf16[32,40,256]{2,1,0:T(8,128)(2,1)S(1)}, u32[]{:S(2)}, u32[]{:S(2)}) async-start(bf16[32,40,256]{2,1,0:T(8,128)(2,1)} %get-tuple-element.25), calls=%async_computation | async-start | bytes 1310720 | tf_op jit(solution)/shard_map/all_to_all | solution.py:363
  20.3 0.0 copy-start
  20.3 0.0 collective-permute-done.other_ref
  20.3 0.0 copy-done.4
  20.4 0.0 copy-start.2
  20.4 0.0 copy-start.3
  20.4 6.2 %all_gather.21.grad_ref = bf16[4,20,512]{2,1,0:T(8,128)(2,1)S(1)} all-gather(bf16[2,20,512]{2,1,0:T(8,128)(2,1)S(1)} %shard_map.94), channel_id=1, replica_groups={{0,3},{1,2},{4,7},{5,6},{8,11},{9,10},{12,15},{13,14},{16,19},{17,18},{..., dimensions={0}, use_global_device_ids=true | all-gather | bytes 122880 | tf_op jit(solution)/shard_map/all_gather | solution.py:372
  26.6 0.0 copy-done
  26.6 0.0 copy-done.2
  26.6 0.0 copy-done.3
  26.6 0.4 shard_map.95
  27.0 0.0 copy-start.1
  27.0 9.7 %all-gather = bf16[96,2560]{1,0:T(8,128)(2,1)S(1)} all-gather(bf16[24,2560]{1,0:T(8,128)(2,1)S(1)} %shard_map.95), channel_id=2, replica_groups={{0,4,32,36},{8,12,40,44},{16,20,48,52},{24,28,56,60},{64,68,96,100},{72..., dimensions={0}, use_global_device_ids=true | all-gather | bytes 614400 | tf_op jit(solution)/shard_map/all_gather | solution.py:376
  36.7 0.0 copy-done.1
  36.7 0.5 shard_map.96
  37.2 0.0 all-to-all-done.kv_ref
  37.2 0.9 %shard_map.97 = (bf16[112,256]{1,0:T(8,128)(2,1)S(1)}, f32[512,128]{1,0:T(8,128)S(1)}, f32[512,128]{1,0:T(8,128)S(1)}, f32[256,64]{1,0:T(8,128)S(1)}, f32[256,64]{1,0:T(8,128)S(1)}) custom-call(bf16[32,40,256]{2,1,0:T(8,128)(2,1)S(1)} %all-to-all-done.kv_ref, bf16[128,256]{1,0:T(8,128)(2,1)S(1)} %get-tuple-element.28.refs_0_, ...), custom_call_target="tpu_custom_call" | custom-call | tf_op jit(solution)/shard_map/pallas_call | solution.py:333
  38.1 8.2 %all-gather.1 = bf16[448,256]{1,0:T(8,128)(2,1)S(1)} all-gather(bf16[112,256]{1,0:T(8,128)(2,1)S(1)} %get-tuple-element.34), channel_id=3, replica_groups={{0,4,32,36},{8,12,40,44},{16,20,48,52},{24,28,56,60},{64,68,96,100},{72..., dimensions={0}, use_global_device_ids=true | all-gather | bytes 286720 | tf_op jit(solution)/shard_map/all_gather | solution.py:394
  46.3 1.6 %shard_map.98 = (bf16[32,56,256]{2,1,0:T(8,128)(2,1)}, bf16[512,128]{1,0:T(8,128)(2,1)S(1)}, bf16[256,64]{1,0:T(8,128)(2,1)S(1)}) custom-call(bf16[4,112,256]{2,1,0:T(8,128)(2,1)S(1)} %bitcast.7, bf16[128,256]{1,0:T(8,128)(2,1)S(1)} %get-tuple-element.28.refs_0_, bf16[128,256]{1,0:T(8,128)(2,1)S(1)} %get-tuple-element.29.refs_1_, ...), custom_call_target="tpu_custom_call" | custom-call | tf_op jit(solution)/shard_map/pallas_call | solution.py:395
  47.9 6.8 %all-to-all-start.1 = ((bf16[32,56,256]{2,1,0:T(8,128)(2,1)}), bf16[32,56,256]{2,1,0:T(8,128)(2,1)S(1)}, u32[]{:S(2)}, u32[]{:S(2)}) async-start(bf16[32,56,256]{2,1,0:T(8,128)(2,1)} %get-tuple-element.42), calls=%async_computation.1 | async-start | bytes 1835008 | tf_op jit(solution)/shard_map/all_to_all | solution.py:404
  54.7 0.2 shard_map.99
  54.9 6.7 %all-gather.2 = f32[384,256]{1,0:T(8,128)S(1)} all-gather(f32[96,256]{1,0:T(8,128)S(1)} %shard_map.99), channel_id=4, replica_groups={{0,4,32,36},{8,12,40,44},{16,20,48,52},{24,28,56,60},{64,68,96,100},{72..., dimensions={0}, use_global_device_ids=true | all-gather | bytes 491520 | tf_op jit(solution)/shard_map/all_gather | solution.py:408
  61.6 0.6 shard_map.100
  62.3 14.1 %all-to-all-done.1.in_ref = bf16[32,56,256]{2,1,0:T(8,128)(2,1)S(1)} async-done(((bf16[32,56,256]{2,1,0:T(8,128)(2,1)}), bf16[32,56,256]{2,1,0:T(8,128)(2,1)S(1)}, u32[]{:S(2)}, u32[]{:S(2)}) %all-to-all-start.1) | async-done | bytes 917536 | tf_op jit(solution)/shard_map/all_to_all | solution.py:404
  76.3 0.7 shard_map.101
  (1 shorter events, 0.0 us)
Async XLA Ops:
  0.6 19.7 %collective-permute-start = (bf16[20,512]{1,0:T(8,128)(2,1)}, bf16[20,512]{1,0:T(8,128)(2,1)S(1)}, u32[]{:S(2)}, u32[]{:S(2)}) collective-permute-start(bf16[20,512]{1,0:T(8,128)(2,1)} %own_ref.1), channel_id=1, source_target_pairs={{0,1},{1,0},{2,3},{3,2},{4,5},{5,4},{6,7},{7,6},{8,9},{9,8},{10,11... | collective-permute-start | bytes 61448 | tf_op jit(solution)/shard_map/ppermute | solution.py:342
  7.4 13.0 %copy-start.4 = (bf16[20,512]{1,0:T(8,128)(2,1)S(1)}, bf16[20,512]{1,0:T(8,128)(2,1)}, u32[]{:S(2)}) copy-start(bf16[20,512]{1,0:T(8,128)(2,1)} %own_ref.1) | copy-start | bytes 61444
  7.4 29.8 %all-to-all-start = ((bf16[32,40,256]{2,1,0:T(8,128)(2,1)}), bf16[32,40,256]{2,1,0:T(8,128)(2,1)S(1)}, u32[]{:S(2)}, u32[]{:S(2)}) async-start(bf16[32,40,256]{2,1,0:T(8,128)(2,1)} %get-tuple-element.25), calls=%async_computation | async-start | bytes 1310720 | tf_op jit(solution)/shard_map/all_to_all | solution.py:363
  20.3 6.2 %copy-start = (bf16[256,2048]{1,0:T(8,128)(2,1)S(1)}, bf16[256,2048]{1,0:T(8,128)(2,1)}, u32[]{:S(2)}) copy-start(bf16[256,2048]{1,0:T(8,128)(2,1)} %weight_ref.1) | copy-start | bytes 3145732
  20.4 6.2 %copy-start.2 = (bf16[20,256]{1,0:T(8,128)(2,1)S(1)}, bf16[20,256]{1,0:T(8,128)(2,1)}, u32[]{:S(2)}) copy-start(bf16[20,256]{1,0:T(8,128)(2,1)} %query_ref.1) | copy-start | bytes 30724
  20.4 6.2 %copy-start.3 = (f32[24,128]{1,0:T(8,128)S(1)}, f32[24,128]{1,0:T(8,128)}, u32[]{:S(2)}) copy-start(f32[24,128]{1,0:T(8,128)} %get-tuple-element.27.live_ref) | copy-start | bytes 36868
  27.0 9.7 %copy-start.1 = (s32[64,128]{1,0:T(8,128)S(1)}, s32[64,128]{1,0:T(8,128)}, u32[]{:S(2)}) copy-start(s32[64,128]{1,0:T(8,128)} %get-tuple-element.26.limit_ref) | copy-start | bytes 98308
  47.9 28.5 %all-to-all-start.1 = ((bf16[32,56,256]{2,1,0:T(8,128)(2,1)}), bf16[32,56,256]{2,1,0:T(8,128)(2,1)S(1)}, u32[]{:S(2)}, u32[]{:S(2)}) async-start(bf16[32,56,256]{2,1,0:T(8,128)(2,1)} %get-tuple-element.42), calls=%async_computation.1 | async-start | bytes 1835008 | tf_op jit(solution)/shard_map/all_to_all | solution.py:404
